TPU v7x, 512 devices: a whole 4x4x16 slice. The times are simulated.
512 devices in a mesh: seg: 64 (over z, x_hi, core), space: 8 (over x_lo, y).
Axes of the slice: x: 4 (x_hi: 2, x_lo: 2; x = x_hi * 2 + x_lo), y: 4, z: 16, core: 2. Of those that a mesh axis runs over, the one named last changes fastest.
Arguments:
- states: float32 [64, 3, 64, 2560], P('seg', None, 'space'), may hold values from -5.25 to 5.25
- tangent_panel: float32 [64, 2, 3, 64, 2560], P('seg', None, None, 'space'), may hold values from -9.3 to 9.3
- wall_inverse: float32 [64, 40, 40], P('space'), may hold values from -0.25 to 0.95
- keep_mask: int32 [64, 64], replicated, may hold values 0 or 1
Outputs:
- corrected: float32 [64, 3, 64, 2560], P('seg', None, 'space')
- new_residual: float32 [64, 3, 64, 2560], P('seg', None, 'space')
All inputs are finite; a program needn't handle non-finite values.
Results may differ from a plain program's by a relative error of at most 0.0004.
Values sent between devices are 32-bit elements; how exact they have to be, the bound alone decides.
A program may use at most 64 MiB of HBM per device.

v0:
```python
import math

import jax
import jax.numpy as jnp
from jax import lax
from jax.sharding import PartitionSpec as P

TIME_STEP = 0.005
VISCOSITY = 0.0025
STREAM_WAVE = 1.0
SPAN_WAVE = 2.0
PRECISE = lax.Precision.HIGHEST


def from_behind(block, axis, distance):
    devices = range(lax.axis_size(axis))
    route = [((i - distance) % len(devices), i) for i in devices]
    return lax.ppermute(block, axis, route)


def fourier_basis(length, stretch):
    indices = jnp.arange(length, dtype=jnp.int32)
    mode_row = indices[:, None]
    point_col = indices[None, :]
    wavenumber = jnp.where(mode_row == length - 1, length // 2, (mode_row + 1) // 2)
    phases = 2.0 * math.pi / length * (wavenumber * point_col % length).astype(jnp.float32)
    boundary = (mode_row == 0) | (mode_row == length - 1)
    amplitude = jnp.where(boundary, math.sqrt(1.0 / length), math.sqrt(2.0 / length))
    is_cosine = (mode_row % 2 == 1) | (mode_row == 0)
    basis_rows = amplitude * jnp.where(is_cosine, jnp.cos(phases), jnp.sin(phases))
    slope_rows = (
        stretch
        * wavenumber.astype(jnp.float32)
        * amplitude
        * jnp.where(is_cosine, -jnp.sin(phases), jnp.cos(phases))
    )
    slope_rows = jnp.where(boundary, jnp.zeros_like(slope_rows), slope_rows)
    return (basis_rows, slope_rows)


def wall_tables(length):
    indices = jnp.arange(1, length + 1, dtype=jnp.int32)
    heights = jnp.cos(math.pi / (length + 1) * indices.astype(jnp.float32))
    row_height = heights[:, None]
    col_height = heights[None, :]
    parity = jnp.where((indices[:, None] + indices[None, :]) % 2 == 0, 1.0, -1.0)
    diagonal_mask = indices[:, None] == indices[None, :]
    spacing = jnp.where(diagonal_mask, 1.0, row_height - col_height)
    derivative = jnp.where(
        diagonal_mask, -row_height / (2.0 * (1.0 - row_height * row_height)), parity / spacing
    )
    return (heights, derivative)


def span_damping(length):
    indices = jnp.arange(length, dtype=jnp.int32)
    wavenumber = jnp.where(indices == length - 1, length // 2, (indices + 1) // 2).astype(
        jnp.float32
    )
    return 1.0 / (1.0 + TIME_STEP * VISCOSITY * (SPAN_WAVE * wavenumber) ** 2)


def along_z(values, matrix):
    return jnp.einsum("fmyk,kz->fmyz", values, matrix, precision=PRECISE)


def along_x(values, matrix):
    return jnp.einsum("fmyz,mx->fxyz", values, matrix, precision=PRECISE)


def along_y(values, matrix):
    return jnp.einsum("ij,fmjk->fmik", matrix, values, precision=PRECISE)


def regroup(values):
    return values.reshape((3, 3) + values.shape[1:])


def forcing(physical, stream_slope, wall_slope, span_slope, heights):
    current = physical[0]
    velocity = heights[None, :, None] + current[0]
    carried = (
        velocity[None, None] * stream_slope
        + current[1][None, None] * wall_slope
        + current[2][None, None] * span_slope
    )
    pushed = (
        physical[:, 0:1] * stream_slope[0][None]
        + physical[:, 1:2] * wall_slope[0][None]
        + physical[:, 2:3] * span_slope[0][None]
    )
    selector = (jnp.arange(3, dtype=jnp.int32) > 0).astype(physical.dtype)[
        :, None, None, None, None
    ]
    tendency = -(carried + selector * pushed)
    return tendency.at[:, 0].add(-physical[:, 1])


def tendency_of(physical, stream_slope, wall_slope, span_slope, heights):
    tendency = forcing(
        regroup(physical), regroup(stream_slope), regroup(wall_slope), regroup(span_slope), heights
    )
    return tendency.reshape(physical.shape)


def implicit_solve(inverse, damping, forced):
    return damping * jnp.einsum("myj,fmjk->fmyk", inverse, forced, precision=PRECISE)


def wall_step(fields, inverse, kept_modes, damping, tables, position):
    stream_basis, stream_deriv, span_basis, span_deriv, heights, wall_deriv = tables
    wall_part = along_y(fields, wall_deriv)
    spectral, spectral_wall = (
        lax.all_to_all(fields, "space", split_axis=2, concat_axis=1, tiled=True),
        lax.all_to_all(wall_part, "space", split_axis=2, concat_axis=1, tiled=True),
    )
    height_band = spectral.shape[2]
    local_heights = lax.dynamic_slice_in_dim(heights, position * height_band, height_band, 0)
    span_part = along_z(spectral, span_basis)
    physical = along_x(span_part, stream_basis)
    stream_slope = along_x(span_part, stream_deriv)
    span_slope = along_x(along_z(spectral, span_deriv), stream_basis)
    wall_slope = along_x(along_z(spectral_wall, span_basis), stream_basis)
    tendency = tendency_of(physical, stream_slope, wall_slope, span_slope, local_heights)
    modes = along_x(along_z(tendency, span_basis.T), stream_basis.T)
    forced = kept_modes[:, None, :] * (spectral + TIME_STEP * modes)
    returned = lax.all_to_all(forced, "space", split_axis=1, concat_axis=2, tiled=True)
    return implicit_solve(inverse, damping, returned)


def local(states, tangent_panel, wall_inverse, keep_mask):
    position = lax.axis_index("space")
    mode_rows = states.shape[2]
    stream_count = keep_mask.shape[0]
    span_count = keep_mask.shape[1]
    wall_count = wall_inverse.shape[1]
    stream_basis, stream_deriv = fourier_basis(stream_count, STREAM_WAVE)
    span_basis, span_deriv = fourier_basis(span_count, SPAN_WAVE)
    heights, wall_deriv = wall_tables(wall_count)
    tables = (stream_basis, stream_deriv, span_basis, span_deriv, heights, wall_deriv)
    kept_modes = keep_mask.astype(jnp.float32)
    damping = span_damping(span_count)
    later_states, later_panel = from_behind((states, tangent_panel), "seg", -1)
    fields = jnp.concatenate([states, tangent_panel[0]], axis=0).reshape(
        9, mode_rows, wall_count, span_count
    )
    fields = wall_step(fields, wall_inverse, kept_modes, damping, tables, position)
    ends = fields.reshape(3, 3, mode_rows, wall_count * span_count)
    finish = ends[0][None]
    image_end = ends[1:][None]
    residual = finish - later_states
    image = image_end - later_panel
    drift = finish - states
    count = lax.axis_size("seg") * states.shape[0] * 3 * stream_count * wall_count * span_count
    inverse_root = 1.0 / math.sqrt(count)
    summed = (0, 2, 3, 4)
    drift_dot = jnp.sum(drift[:, None] * tangent_panel, axis=summed)
    self_dot = jnp.sum(image * image, axis=summed)
    aim_dot = jnp.sum(image * residual[:, None], axis=summed)
    drift_dot, self_dot, aim_dot = lax.psum((drift_dot, self_dot, aim_dot), ("seg", "space"))
    border = drift_dot * inverse_root
    diag = self_dot + border * border
    first = -aim_dot / diag
    moved = residual + first[0] * image[:, 0] + first[1] * image[:, 1]
    lift = jnp.sum(border * first)
    moved_dot = lax.psum(jnp.sum(image * moved[:, None], axis=summed), ("seg", "space"))
    second_aim = moved_dot + border * lift
    second = -second_aim / diag
    new_residual = moved + second[0] * image[:, 0] + second[1] * image[:, 1]
    combined = first + second
    corrected = states + combined[0] * tangent_panel[:, 0] + combined[1] * tangent_panel[:, 1]
    return (corrected, new_residual)


def solution(mesh):
    return jax.shard_map(
        local,
        mesh=mesh,
        in_specs=(
            P("seg", None, "space", None),
            P("seg", None, None, "space", None),
            P("space", None, None),
            P(),
        ),
        out_specs=(P("seg", None, "space", None), P("seg", None, "space", None)),
        check_vma=False,
    )
```

profile of v0, /device:TPU:1, one launch (start us, length us, event | category | flops | bytes accessed | tf_op | source)
XLA Modules:
  0.0 313.4 jit_solution(7336986021811946259)
XLA Ops:
  2.4 1.8 reshape.341
  4.2 5.9 %all-to-all-start = ((f32[8,1,23040]{2,1,0:T(1,128)}), f32[8,1,23040]{2,1,0:T(1,128)S(1)}, u32[]{:S(2)}, u32[]{:S(2)}) async-start(f32[8,1,23040]{2,1,0:T(1,128)} %reshape.341), calls=%async_computation | async-start | bytes 1474560 | tf_op jit(solution)/shard_map/all_to_all | solution.py:114
  12.0 1.8 reshape.343
  13.9 4.4 %all-to-all-done = f32[8,1,23040]{2,1,0:T(1,128)S(1)} async-done(((f32[8,1,23040]{2,1,0:T(1,128)}), f32[8,1,23040]{2,1,0:T(1,128)S(1)}, u32[]{:S(2)}, u32[]{:S(2)}) %all-to-all-start) | async-done | bytes 737312 | tf_op jit(solution)/shard_map/all_to_all | solution.py:114
  18.3 4.4 %all-to-all-start.1 = ((f32[8,1,23040]{2,1,0:T(1,128)}), f32[8,1,23040]{2,1,0:T(1,128)}, u32[]{:S(2)}, u32[]{:S(2)}) async-start(f32[8,1,23040]{2,1,0:T(1,128)} %reshape.343), calls=%async_computation.1 | async-start | bytes 1474560 | tf_op jit(solution)/shard_map/all_to_all | solution.py:115
  23.2 2.4 reduce.2
  31.4 4.4 %reduce.3 = f32[8,23040]{1,0:T(8,128)} reduce(f32[8,1,23040]{2,1,0:T(1,128)} %all-to-all-done.1, f32[]{:T(128)} %broadcast.566), dimensions={1}, to_apply=%all_to_all.43.reduce_sub_computation | reduce | bytes 1474564 | tf_op jit(solution)/shard_map/all_to_all | solution.py:115
  35.8 2.5 reshape.344
  38.3 2.9 fusion.1
  42.8 1.8 fusion.22
  51.8 1.7 fusion
  54.4 1.9 reshape.345
  56.3 4.9 %all-to-all-start.2 = ((f32[8,1,23040]{2,1,0:T(1,128)}), f32[8,1,23040]{2,1,0:T(1,128)S(1)}, u32[]{:S(2)}, u32[]{:S(2)}) async-start(f32[8,1,23040]{2,1,0:T(1,128)} %reshape.345), calls=%async_computation.2 | async-start | bytes 1474560 | tf_op jit(solution)/shard_map/all_to_all | solution.py:127
  61.2 8.0 %collective-permute-start.1 = (f32[1,3,8,2560]{3,2,1,0:T(8,128)}, f32[1,3,8,2560]{3,2,1,0:T(8,128)}, u32[]{:S(2)}, u32[]{:S(2)}) collective-permute-start(f32[1,3,8,2560]{3,2,1,0:T(8,128)} %param.6), channel_id=1, source_target_pairs={{8,0},{16,8},{24,16},{32,24},{40,32},{48,40},{56,48},{64,56},{72,6... | collective-permute-start | bytes 737288 | tf_op jit(solution)/shard_map/ppermute | solution.py:18
  69.1 12.5 %collective-permute-start = (f32[1,2,3,8,2560]{4,3,2,1,0:T(8,128)S(1)}, f32[1,2,3,8,2560]{4,3,2,1,0:T(8,128)}, u32[]{:S(2)}, u32[]{:S(2)}) collective-permute-start(f32[1,2,3,8,2560]{4,3,2,1,0:T(8,128)S(1)} %copy-done.2), channel_id=1, source_target_pairs={{8,0},{16,8},{24,16},{32,24},{40,32},{48,40},{56,48},{64,56},{72,6... | collective-permute-start | bytes 1474568 | tf_op jit(solution)/shard_map/ppermute | solution.py:18
  81.6 3.4 %reduce.4 = f32[8,23040]{1,0:T(8,128)} reduce(f32[8,1,23040]{2,1,0:T(1,128)S(1)} %all-to-all-done.2, f32[]{:T(128)} %broadcast.566), dimensions={1}, to_apply=%all_to_all.47.reduce_sub_computation | reduce | bytes 1474564 | tf_op jit(solution)/shard_map/all_to_all | solution.py:127
  85.1 1.8 reshape.346
  87.2 1.6 multiply_bitcast_fusion
  89.1 1.9 subtract_bitcast_fusion
  93.7 110.5 %all-reduce = (f32[2]{0:T(128)S(1)}, f32[2]{0:T(128)S(1)}, f32[2]{0:T(128)S(1)}) all-reduce(f32[2]{0:T(128)S(1)} %get-tuple-element.15, f32[2]{0:T(128)S(1)} %get-tuple-element.14, f32[2]{0:T(128)S(1)} %multiply_reduce_fusion.1), channel_id=1, replica_groups=mesh['seg'=64,'space'=8] {'seg','space'}, use_global_device_ids=true, to_apply=%region_1.2 | all-reduce | flops 6 | bytes 48 | tf_op jit(solution)/shard_map/psum | solution.py:160
  205.5 2.3 bitcast_add_fusion.5
  207.9 98.7 %psum.31 = f32[2]{0:T(128)S(1)} all-reduce(f32[2]{0:T(128)S(1)} %multiply_reduce_fusion), channel_id=1, replica_groups=mesh['seg'=64,'space'=8] {'seg','space'}, use_global_device_ids=true, to_apply=%region_7.8 | all-reduce | flops 2 | bytes 16 | tf_op jit(solution)/shard_map/psum | solution.py:166
  308.6 2.0 bitcast_add_fusion.1
  310.6 2.9 bitcast_add_fusion.3
  (70 shorter events, 25.3 us)
Async XLA Ops:
  0.6 86.6 %copy-start = (f32[8,40,40]{2,1,0:T(8,128)S(1)}, f32[8,40,40]{2,1,0:T(8,128)}, u32[]{:S(2)}) copy-start(f32[8,40,40]{2,1,0:T(8,128)} %param.8) | copy-start | bytes 153604
  4.2 14.1 %all-to-all-start = ((f32[8,1,23040]{2,1,0:T(1,128)}), f32[8,1,23040]{2,1,0:T(1,128)S(1)}, u32[]{:S(2)}, u32[]{:S(2)}) async-start(f32[8,1,23040]{2,1,0:T(1,128)} %reshape.341), calls=%async_computation | async-start | bytes 1474560 | tf_op jit(solution)/shard_map/all_to_all | solution.py:114
  12.0 1.8 copy-start.9
  18.3 13.1 %all-to-all-start.1 = ((f32[8,1,23040]{2,1,0:T(1,128)}), f32[8,1,23040]{2,1,0:T(1,128)}, u32[]{:S(2)}, u32[]{:S(2)}) async-start(f32[8,1,23040]{2,1,0:T(1,128)} %reshape.343), calls=%async_computation.1 | async-start | bytes 1474560 | tf_op jit(solution)/shard_map/all_to_all | solution.py:115
  29.0 1.2 copy-start.1
  46.3 1.7 copy-start.3
  46.3 1.7 copy-start.4
  46.3 1.7 copy-start.5
  46.3 1.7 copy-start.8
  54.4 14.7 %copy-start.2 = (f32[1,2,3,8,2560]{4,3,2,1,0:T(8,128)S(1)}, f32[1,2,3,8,2560]{4,3,2,1,0:T(8,128)}, u32[]{:S(2)}) copy-start(f32[1,2,3,8,2560]{4,3,2,1,0:T(8,128)} %param.7) | copy-start | bytes 1474564
  56.3 25.3 %all-to-all-start.2 = ((f32[8,1,23040]{2,1,0:T(1,128)}), f32[8,1,23040]{2,1,0:T(1,128)S(1)}, u32[]{:S(2)}, u32[]{:S(2)}) async-start(f32[8,1,23040]{2,1,0:T(1,128)} %reshape.345), calls=%async_computation.2 | async-start | bytes 1474560 | tf_op jit(solution)/shard_map/all_to_all | solution.py:127
  61.2 28.0 %collective-permute-start.1 = (f32[1,3,8,2560]{3,2,1,0:T(8,128)}, f32[1,3,8,2560]{3,2,1,0:T(8,128)}, u32[]{:S(2)}, u32[]{:S(2)}) collective-permute-start(f32[1,3,8,2560]{3,2,1,0:T(8,128)} %param.6), channel_id=1, source_target_pairs={{8,0},{16,8},{24,16},{32,24},{40,32},{48,40},{56,48},{64,56},{72,6... | collective-permute-start | bytes 737288 | tf_op jit(solution)/shard_map/ppermute | solution.py:18
  69.1 23.2 %collective-permute-start = (f32[1,2,3,8,2560]{4,3,2,1,0:T(8,128)S(1)}, f32[1,2,3,8,2560]{4,3,2,1,0:T(8,128)}, u32[]{:S(2)}, u32[]{:S(2)}) collective-permute-start(f32[1,2,3,8,2560]{4,3,2,1,0:T(8,128)S(1)} %copy-done.2), channel_id=1, source_target_pairs={{8,0},{16,8},{24,16},{32,24},{40,32},{48,40},{56,48},{64,56},{72,6... | collective-permute-start | bytes 1474568 | tf_op jit(solution)/shard_map/ppermute | solution.py:18
  91.1 0.9 copy-start.7
  91.2 1.1 copy-start.6
where the time goes:
time: 314 us; the launch traced here: 313 us
  blocking collectives  209 us (67%)
  starting transfers between devices  35.6 us (11%)
  other arithmetic  26.1 us (8%)
  matrix products  18.7 us (6%)
  local copies, waits for them, and re-layouts  17.6 us (6%)
  waiting for transfers between devices  4.42 us (1%)
    psum x1, blocking collectives, local(): lax.psum((drift_dot, self_dot, aim_dot), ('seg', 'space'))  111 us
    psum x1, blocking collectives, local(): lax.psum(jnp.sum(image * moved[:, None], axis=summed), ('seg', 'space'))  98.7 us
    ppermute x2, starting transfers between devices, from_behind(): return lax.ppermute(block, axis, route)  20.4 us
    unnamed x26, local copies, waits for them, and re-layouts  11 us
    dot_general x5, matrix products, along_x(): return jnp.einsum('fmyz,mx->fxyz', values, matrix, precision=PRECISE)  8.29 us
    dot_general x4, matrix products, along_z(): return jnp.einsum('fmyk,kz->fmyz', values, matrix, precision=PRECISE)  7.4 us
  transfers between devices with their start and end apart: 5, of which 1 were waited for; matrix products, arithmetic and copies ran while one was open for 7% of the time, Pallas kernels for 0%

commit v1 on v0

v1 whole, which is shorter than its diff:
```python
import functools
import math

import jax
import jax.numpy as jnp
import ml_dtypes
import numpy as np
from jax import lax
from jax.experimental import pallas as pl
from jax.experimental.pallas import tpu as pltpu
from jax.sharding import PartitionSpec as P

TIME_STEP = 0.005
VISCOSITY = 0.0025
STREAM_WAVE = 1.0
SPAN_WAVE = 2.0
MESH = pl.DeviceIdType.MESH
NX, NY, NZ = 64, 40, 64
TILE = 128
PAIRS = NY // 2
LANES = NY * NZ


def fourier_basis(length, stretch):
    mode = np.arange(length)[:, None]
    point = np.arange(length)[None, :]
    wave = np.where(mode == length - 1, length // 2, (mode + 1) // 2)
    phase = 2.0 * math.pi / length * (wave * point % length)
    edge = (mode == 0) | (mode == length - 1)
    amplitude = np.where(edge, math.sqrt(1.0 / length), math.sqrt(2.0 / length))
    cosine = (mode % 2 == 1) | (mode == 0)
    basis = amplitude * np.where(cosine, np.cos(phase), np.sin(phase))
    slope = stretch * wave * amplitude * np.where(cosine, -np.sin(phase), np.cos(phase))
    return basis, np.where(edge, 0.0, slope)


def wall_tables(length):
    index = np.arange(1, length + 1)
    height = np.cos(math.pi / (length + 1) * index)
    row, col = height[:, None], height[None, :]
    parity = np.where((index[:, None] + index[None, :]) % 2 == 0, 1.0, -1.0)
    same = index[:, None] == index[None, :]
    spacing = np.where(same, 1.0, row - col)
    return height, np.where(same, -row / (2.0 * (1.0 - row * row)), parity / spacing)


def span_damping(length):
    index = np.arange(length)
    wave = np.where(index == length - 1, length // 2, (index + 1) // 2)
    return 1.0 / (1.0 + TIME_STEP * VISCOSITY * (SPAN_WAVE * wave) ** 2)


def parts(matrix):
    high = matrix.astype(np.float32).astype(ml_dtypes.bfloat16)
    low = (matrix - high.astype(np.float64)).astype(np.float32).astype(ml_dtypes.bfloat16)
    return high, low


def twice(matrix):
    zero = np.zeros_like(matrix)
    return np.block([[matrix, zero], [zero, matrix]])


def tables():
    qx, sx = fourier_basis(NX, STREAM_WAVE)
    qz, sz = fourier_basis(NZ, SPAN_WAVE)
    height, wall = wall_tables(NY)
    high, low = parts(np.concatenate([qx.T, sx.T], axis=0))
    x_forward = np.concatenate([high, high, low], axis=1)
    high, low = parts(qx)
    x_back = np.concatenate([high, high, low], axis=1)
    high, low = parts(np.concatenate([twice(qz), twice(sz)], axis=1))
    z_forward = np.concatenate([high, high, low], axis=0)
    high, low = parts(-TIME_STEP * twice(qz.T))
    z_back = np.concatenate([high, high, low], axis=0)
    derivative = np.zeros((PAIRS, 2 * PAIRS, TILE))
    for half in (0, 1):
        lanes = slice(half * NZ, (half + 1) * NZ)
        derivative[:, 0::2, lanes] = wall[half::2, half::2][:, :, None]
        derivative[:, 1::2, lanes] = wall[half::2, 1 - half :: 2][:, :, None]
    heights = np.repeat(height.reshape(PAIRS, 1, 2), NZ, axis=2)
    damping = np.tile(span_damping(NZ), 2)[None, :]
    single = [value.astype(np.float32) for value in (derivative, heights, damping)]
    return (x_forward, x_back, z_forward, z_back, *single)


def band(place):
    row, side = lax.rem(place, 4), lax.div(place, 4)
    odd = lax.rem(row, 2)
    count = 3 - lax.rem(row + side, 2)
    return 5 * row + side * (3 - odd), count


def tile_at(index, tiles=1):
    return pl.ds(pl.multiple_of(index * TILE, TILE), tiles * TILE)


def split(value):
    high = value.astype(jnp.bfloat16)
    low = (value - high.astype(jnp.float32)).astype(jnp.bfloat16)
    return high, low


def stacked(value, axis):
    high, low = split(value)
    return jnp.concatenate([high, low, high], axis=axis)


def mul(a, b):
    return jnp.dot(a, b, preferred_element_type=jnp.float32)


def kernel(
    nseg,
    states,
    panel,
    wall,
    mask,
    x_forward_in,
    x_back_in,
    z_forward_in,
    z_back_in,
    derivative_in,
    heights_in,
    damping_in,
    corrected,
    new_residual,
    x_forward,
    x_back,
    z_forward,
    z_back,
    derivative,
    heights,
    damping,
    wall_v,
    mask_v,
    fields,
    swapped,
    slopes,
    got,
    flow,
    outgoing,
    returned,
    solve,
    forced,
    turned,
    ends,
    later,
    near,
    far,
    in_sem,
    out_send,
    out_recv,
    back_send,
    back_recv,
    later_send,
    later_recv,
    sum_send,
    sum_recv,
):
    seg = lax.axis_index("seg")
    place = lax.axis_index("space")
    core = lax.rem(seg, 2)
    chip_pair = lax.div(seg, 2)
    before = lax.rem(seg + nseg - 1, nseg)
    across = lax.rem(seg + nseg + 2 * core - 1, nseg)
    near_count, far_count = 16, nseg // 2
    near_me = core * 8 + place
    first_pair, count = band(place)

    def near_device(step):
        other = lax.rem(near_me + step, near_count)
        return (seg - core + lax.div(other, 8), lax.rem(other, 8))

    def far_device(step):
        return (2 * lax.rem(chip_pair + step, far_count) + core, place)

    barrier = pltpu.get_barrier_semaphore()
    for step in range(1, near_count):
        pl.semaphore_signal(barrier, inc=1, device_id=near_device(step), device_id_type=MESH)
    pl.semaphore_signal(barrier, inc=1, device_id=(across, place), device_id_type=MESH)
    for step in range(1, far_count):
        pl.semaphore_signal(barrier, inc=1, device_id=far_device(step), device_id_type=MESH)

    loads = [
        (states.at[0], fields.at[pl.ds(0, 3)]),
        (panel.at[0, 0], fields.at[pl.ds(3, 3)]),
        (panel.at[0, 1], fields.at[pl.ds(6, 3)]),
        (derivative_in, derivative),
        (wall, wall_v),
        (mask, mask_v),
        (x_forward_in, x_forward),
        (z_forward_in, z_forward),
        (x_back_in, x_back),
        (z_back_in, z_back),
        (heights_in, heights),
        (damping_in, damping),
    ]
    loads = [
        pltpu.make_async_copy(src, dst, in_sem.at[index])
        for index, (src, dst) in enumerate(loads)
    ]
    for load in loads:
        load.start()
    pl.semaphore_wait(barrier, near_count + far_count - 1)

    def send_heights(unit, group, source):
        for step in range(1, 8):
            other = lax.rem(place + step, 8)
            other_first, other_count = band(other)
            pltpu.make_async_remote_copy(
                src_ref=source.at[:, :, tile_at(other_first, 2)],
                dst_ref=got.at[unit, group, :, place, :, pl.ds(0, 2 * TILE)],
                send_sem=out_send.at[unit, group],
                recv_sem=out_recv.at[unit, group],
                device_id=(seg, other),
                device_id_type=MESH,
            ).start()

            @pl.when(other_count == 3)
            def _():
                pltpu.make_async_remote_copy(
                    src_ref=source.at[:, :, tile_at(other_first + 2)],
                    dst_ref=got.at[unit, group, :, place, :, pl.ds(2 * TILE, TILE)],
                    send_sem=out_send.at[unit, group],
                    recv_sem=out_recv.at[unit, group],
                    device_id=(seg, other),
                    device_id_type=MESH,
                ).start()

    def keep_heights(unit, group, source):
        got[unit, group, :, place, :, pl.ds(0, 2 * TILE)] = source[
            pl.ds(3 * group, 3), :, tile_at(first_pair, 2)
        ]

        @pl.when(count == 3)
        def _():
            got[unit, group, :, place, :, pl.ds(2 * TILE, TILE)] = source[
                pl.ds(3 * group, 3), :, tile_at(first_pair + 2)
            ]

    def drain(ref, sem):
        pltpu.make_async_copy(ref, ref, sem).wait()

    def wait_heights(unit, group):
        @pl.when(count == 3)
        def _():
            drain(
                got.at[unit, group, :, pl.ds(0, 7), :, pl.ds(0, 3 * TILE)],
                out_recv.at[unit, group],
            )

        @pl.when(count == 2)
        def _():
            drain(
                got.at[unit, group, :, pl.ds(0, 7), :, pl.ds(0, 2 * TILE)],
                out_recv.at[unit, group],
            )

    def wait_pairs(sem):
        @pl.when(count == 3)
        def _():
            drain(returned.at[0, :, :, pl.ds(0, (PAIRS - 3) * TILE)], sem)

        @pl.when(count == 2)
        def _():
            drain(returned.at[0, :, :, pl.ds(0, (PAIRS - 2) * TILE)], sem)

    def across_heights(group, source, other, coefficient, target):
        rows = pl.ds(3 * group, 3)

        def step(index, carry):
            sums = [jnp.zeros((3, 8, TILE), jnp.float32) for _ in range(2)]
            for pair in range(PAIRS):
                lanes = pl.ds(pair * TILE, TILE)
                straight, turned_pair = source[rows, :, lanes], other[rows, :, lanes]
                for which in range(2):
                    sums[which] += coefficient(2 * index + which, 2 * pair) * straight
                    sums[which] += coefficient(2 * index + which, 2 * pair + 1) * turned_pair
            target[rows, :, tile_at(2 * index)] = sums[0]
            target[rows, :, tile_at(2 * index + 1)] = sums[1]
            return carry

        lax.fori_loop(0, PAIRS // 2, step, 0)

    def turn(group, source, target):
        rows = pl.ds(3 * group, 3)
        for pair in range(PAIRS):
            lanes = pl.ds(pair * TILE, TILE)
            target[rows, :, lanes] = pltpu.roll(source[rows, :, lanes], NZ, 2)

    for group in range(3):
        source = states.at[0] if group == 0 else panel.at[0, group - 1]
        send_heights(0, group, source)
        loads[group].wait()
        if group == 0:
            loads[3].wait()
        turn(group, fields, swapped)
        across_heights(
            group,
            fields,
            swapped,
            lambda pair, row: derivative[pair, pl.ds(row, 1), :],
            slopes,
        )
        send_heights(1, group, slopes.at[pl.ds(3 * group, 3)])
        keep_heights(0, group, fields)
        keep_heights(1, group, slopes)

    shift = [
        pltpu.make_async_remote_copy(
            src_ref=src,
            dst_ref=dst,
            send_sem=later_send.at[index],
            recv_sem=later_recv.at[index],
            device_id=(before, place),
            device_id_type=MESH,
        )
        for index, (src, dst) in enumerate(
            [
                (states.at[0], later.at[pl.ds(0, 3)]),
                (panel.at[0, 0], later.at[pl.ds(3, 3)]),
                (panel.at[0, 1], later.at[pl.ds(6, 3)]),
            ]
        )
    ]
    for copy in shift:
        copy.start()
    for load in loads[4:]:
        load.wait()

    lane = lax.broadcasted_iota(jnp.int32, (8, TILE), 1)
    low_half = lane < NZ

    def solve_rows(pair, carry):
        even = wall_v[pl.ds(2 * pair, 8, stride=NY), :]
        odd = wall_v[pl.ds(2 * pair + 1, 8, stride=NY), :]

        def spread(value, column):
            return jnp.broadcast_to(value[:, column : column + 1], (8, TILE))

        for other in range(PAIRS):
            solve[pair, 2 * other] = jnp.where(
                low_half, spread(even, 2 * other), spread(odd, 2 * other + 1)
            )
            solve[pair, 2 * other + 1] = jnp.where(
                low_half, spread(even, 2 * other + 1), spread(odd, 2 * other)
            )
        return carry

    lax.fori_loop(0, PAIRS, solve_rows, 0)

    own_rows = mask_v[pl.ds(pl.multiple_of(place * 8, 8), 8), :].astype(jnp.float32)
    keep = jnp.concatenate([own_rows, own_rows], axis=1) * damping[...]

    def transform(group):
        def step(index, carry):
            lanes = tile_at(index)

            def modes(unit):
                value = got[unit, group, :, :, :, lanes]
                value = value.reshape(3, NX, TILE)
                return stacked(jnp.concatenate([value[0], value[1], value[2]], axis=1), 0)

            def by_rows(value):
                return [value[:, c * TILE : (c + 1) * TILE] for c in range(3)]

            in_x = mul(x_forward[...], modes(0))
            in_x_wall = mul(x_forward[pl.ds(0, NX), :], modes(1))
            plain = jnp.concatenate(by_rows(in_x[:NX]), axis=0)
            rest = jnp.concatenate(by_rows(in_x[NX:]) + by_rows(in_x_wall), axis=0)
            pair = mul(stacked(plain, 1), z_forward[...])
            single = mul(stacked(rest, 1), z_forward[:, pl.ds(0, TILE)])

            def field(value, c):
                return value[c * NX : (c + 1) * NX]

            physical = [field(pair[:, :TILE], c) for c in range(3)]
            span = [field(pair[:, TILE:], c) for c in range(3)]
            stream = [field(single, c) for c in range(3)]
            slope = [field(single, c + 3) for c in range(3)]
            if group == 0:
                for c in range(3):
                    flow[index, c] = physical[c]
                    flow[index, 3 + c] = stream[c]
                    flow[index, 6 + c] = slope[c]
                    flow[index, 9 + c] = span[c]
                u, v, w = physical
            else:
                u, v, w = (flow[index, c] for c in range(3))
            u = u + heights[first_pair + index]
            total = []
            for c in range(3):
                value = u * stream[c] + v * slope[c] + w * span[c]
                if group > 0:
                    value += (
                        physical[0] * flow[index, 3 + c]
                        + physical[1] * flow[index, 6 + c]
                        + physical[2] * flow[index, 9 + c]
                    )
                if c == 0:
                    value += physical[1]
                total.append(value)
            in_k = mul(stacked(jnp.concatenate(total, axis=0), 1), z_back[...])
            in_k = jnp.concatenate([field(in_k, c) for c in range(3)], axis=1)
            in_m = mul(x_back[...], stacked(in_k, 0))
            for c in range(3):
                outgoing[group, index, c] = in_m[:, c * TILE : (c + 1) * TILE]
            spot = tile_at(first_pair + index)
            for hop in range(1, 8):
                other = lax.rem(place + hop, 8)
                pltpu.make_async_remote_copy(
                    src_ref=outgoing.at[
                        group, index, :, pl.ds(pl.multiple_of(other * 8, 8), 8), :
                    ],
                    dst_ref=returned.at[group, :, :, spot],
                    send_sem=back_send.at[group],
                    recv_sem=back_recv.at[group],
                    device_id=(seg, other),
                    device_id_type=MESH,
                ).start()
            returned[group, :, :, spot] = outgoing[
                group, index, :, pl.ds(pl.multiple_of(place * 8, 8), 8), :
            ]
            return carry

        wait_heights(0, group)
        wait_heights(1, group)
        lax.fori_loop(0, count, step, 0)

    def finish(group):
        wait_pairs(back_recv.at[group])
        rows = pl.ds(3 * group, 3)
        for pair in range(PAIRS):
            lanes = pl.ds(pair * TILE, TILE)
            value = keep * (fields[rows, :, lanes] + returned[group, :, :, lanes])
            forced[rows, :, lanes] = value
            turned[rows, :, lanes] = pltpu.roll(value, NZ, 2)
        across_heights(
            group, forced, turned, lambda pair, row: solve[pair, row], ends
        )

    transform(0)
    transform(1)
    finish(0)
    transform(2)
    finish(1)
    for copy in shift:
        copy.wait_recv()
    finish(2)

    def products(index, sums):
        lanes = tile_at(index)
        start = [fields[pl.ds(3 * g, 3), :, lanes] for g in range(3)]
        end = [ends[pl.ds(3 * g, 3), :, lanes] for g in range(3)]
        gap = [end[g] - later[pl.ds(3 * g, 3), :, lanes] for g in range(3)]
        for g in range(3):
            ends[pl.ds(3 * g, 3), :, lanes] = gap[g]
        drift = end[0] - start[0]
        terms = [
            drift * start[1],
            drift * start[2],
            gap[1] * gap[1],
            gap[2] * gap[2],
            gap[1] * gap[0],
            gap[2] * gap[0],
            gap[1] * gap[2],
        ]
        return tuple(s + t[0] + t[1] + t[2] for s, t in zip(sums, terms))

    sums = lax.fori_loop(
        0, PAIRS, products, tuple(jnp.zeros((8, TILE), jnp.float32) for _ in range(7))
    )
    row = lax.broadcasted_iota(jnp.int32, (1, TILE), 1)
    message = jnp.zeros((1, TILE), jnp.float32)
    for index, value in enumerate(sums):
        total = jnp.sum(jnp.sum(value, axis=0, keepdims=True), axis=1, keepdims=True)
        message = jnp.where(row == index, total, message)

    def exchange(which, slots, me, size, device, value):
        slots[me] = value
        for step in range(1, size):
            pltpu.make_async_remote_copy(
                src_ref=slots.at[me],
                dst_ref=slots.at[me],
                send_sem=sum_send.at[which],
                recv_sem=sum_recv.at[which],
                device_id=device(step),
                device_id_type=MESH,
            ).start()
        if size > 1:
            drain(slots.at[pl.ds(0, size - 1)], sum_recv.at[which])
        return jnp.sum(slots[...], axis=0)

    message = exchange(0, near, near_me, near_count, near_device, message)
    message = exchange(1, far, chip_pair, far_count, far_device, message)

    def number(index):
        return message[:, index : index + 1]

    root = 1.0 / math.sqrt(nseg * 3 * NX * LANES)
    border = [number(0) * root, number(1) * root]
    diag = [number(2) + border[0] * border[0], number(3) + border[1] * border[1]]
    first = [-number(4) / diag[0], -number(5) / diag[1]]
    cross = number(6) + border[0] * border[1]
    weight = [
        first[0] - first[1] * cross / diag[0],
        first[1] - first[0] * cross / diag[1],
    ]
    weight = [jnp.broadcast_to(value, (8, TILE)) for value in weight]

    def write(index, carry):
        lanes = tile_at(index)
        for source, target in ((fields, corrected), (ends, new_residual)):
            target[0, :, :, lanes] = (
                source[pl.ds(0, 3), :, lanes]
                + weight[0] * source[pl.ds(3, 3), :, lanes]
                + weight[1] * source[pl.ds(6, 3), :, lanes]
            )
        return carry

    lax.fori_loop(0, PAIRS, write, 0)

    for unit in range(2):
        for group in range(3):
            wait_pairs(out_send.at[unit, group])
    for group in range(3):
        @pl.when(count == 3)
        def _():
            drain(outgoing.at[group, pl.ds(0, 3), :, pl.ds(0, 56), :], back_send.at[group])

        @pl.when(count == 2)
        def _():
            drain(outgoing.at[group, pl.ds(0, 2), :, pl.ds(0, 56), :], back_send.at[group])

    for copy in shift:
        copy.wait_send()
    drain(near.at[pl.ds(0, near_count - 1)], sum_send.at[0])
    if far_count > 1:
        drain(far.at[pl.ds(0, far_count - 1)], sum_send.at[1])


def local(nseg, constants, states, tangent_panel, wall_inverse, keep_mask):
    operands = (
        states,
        tangent_panel,
        wall_inverse.reshape(8 * NY, NY),
        keep_mask,
        *[jnp.asarray(value) for value in constants],
    )
    f32 = jnp.float32
    sem = pltpu.SemaphoreType.DMA
    whole = (9, 8, LANES)
    scratch = [
        *[pltpu.VMEM(value.shape, value.dtype) for value in constants],
        pltpu.VMEM((8 * NY, NY), f32),
        pltpu.VMEM((NX, NZ), jnp.int32),
        pltpu.VMEM(whole, f32),
        pltpu.VMEM(whole, f32),
        pltpu.VMEM(whole, f32),
        pltpu.VMEM((2, 3, 3, 8, 8, 3 * TILE), f32),
        pltpu.VMEM((3, 12, NX, TILE), f32),
        pltpu.VMEM((3, 3, 3, NX, TILE), f32),
        pltpu.VMEM((3, 3, 8, LANES), f32),
        pltpu.VMEM((PAIRS, 2 * PAIRS, 8, TILE), f32),
        pltpu.VMEM(whole, f32),
        pltpu.VMEM(whole, f32),
        pltpu.VMEM(whole, f32),
        pltpu.VMEM(whole, f32),
        pltpu.VMEM((16, 1, TILE), f32),
        pltpu.VMEM((nseg // 2, 1, TILE), f32),
        sem((12,)),
        sem((2, 3)),
        sem((2, 3)),
        sem((3,)),
        sem((3,)),
        sem((3,)),
        sem((3,)),
        sem((2,)),
        sem((2,)),
    ]
    return pl.pallas_call(
        functools.partial(kernel, nseg),
        out_shape=[jax.ShapeDtypeStruct((1, 3, 8, LANES), f32)] * 2,
        in_specs=[pl.BlockSpec(memory_space=pl.ANY)] * len(operands),
        out_specs=[pl.BlockSpec(memory_space=pltpu.VMEM)] * 2,
        scratch_shapes=scratch,
        compiler_params=pltpu.CompilerParams(
            collective_id=0, has_side_effects=True, vmem_limit_bytes=48 * 1024 * 1024
        ),
        name="newton_step",
    )(*operands)


def solution(mesh):
    return jax.shard_map(
        functools.partial(local, mesh.shape["seg"], tables()),
        mesh=mesh,
        in_specs=(
            P("seg", None, "space", None),
            P("seg", None, None, "space", None),
            P("space", None, None),
            P(),
        ),
        out_specs=(P("seg", None, "space", None), P("seg", None, "space", None)),
        check_vma=False,
    )
```

time: 314 us -> 84.6 us (0.27)
  blocking collectives: 209 us -> 0 us
  Pallas kernels: 0 us -> 73.2 us
  starting transfers between devices: 35.6 us -> 0 us
  other arithmetic: 26.1 us -> 0 us
  matrix products: 18.7 us -> 0 us
  local copies, waits for them, and re-layouts: 17.6 us -> 10.1 us
  waiting for transfers between devices: 4.42 us -> 0 us
    psum x2 -> x0, blocking collectives: 209 us -> none  [the longest x1 111 us: local(): lax.psum((drift_dot, self_dot, aim_dot), ('seg', 'space'))]
    pallas_call x0 -> x1, Pallas kernels: none -> 73.2 us  [local(): pl.pallas_call(functools.partial(kernel, nseg), out_shape=[jax.ShapeDtype...]
    ppermute x2 -> x0, starting transfers between devices: 20.4 us -> none  [from_behind(): return lax.ppermute(block, axis, route)]
    dot_general x11 -> x0, matrix products: 18.7 us -> none  [the longest x5 8.29 us: along_x(): return jnp.einsum('fmyz,mx->fxyz', values, matrix, precision=PRECISE)]
    all_to_all x3 -> x0, starting transfers between devices: 15.2 us -> none  [the longest x1 5.95 us: wall_step(): lax.all_to_all(fields, 'space', split_axis=2, concat_axis=1, tiled=True)]
    all_to_all x3 -> x0, other arithmetic: 10.2 us -> none  [the longest x1 4.37 us: wall_step(): lax.all_to_all(wall_part, 'space', split_axis=2, concat_axis=1, tiled=True)]
    add x6 -> x0, other arithmetic: 7.99 us -> none  [the longest x1 2.87 us: local(): states + combined[0] * tangent_panel[:, 0]]
    all_to_all x3 -> x0, waiting for transfers between devices: 4.42 us -> none  [the longest x1 4.41 us: wall_step(): lax.all_to_all(fields, 'space', split_axis=2, concat_axis=1, tiled=True)]
  transfers between devices with their start and end apart: 5 -> 0, of which waited for: 1 -> 0; matrix products, arithmetic and copies ran while one was open for 7% -> 0% of each run, Pallas kernels for 0% -> 0%
where the time goes in v1:
time: 84.6 us; the launch traced here: 84.1 us
  Pallas kernels  73.2 us (87%)
  local copies, waits for them, and re-layouts  10.1 us (12%)
    pallas_call x1, Pallas kernels, local(): pl.pallas_call(functools.partial(kernel, nseg), out_shape=[jax.ShapeDtype...  73.2 us
    unnamed x24, local copies, waits for them, and re-layouts  10.1 us

profile of v1, /device:TPU:1, one launch (start us, length us, event | category | flops | bytes accessed | tf_op | source)
XLA Modules:
  0.0 84.1 jit_solution(3993932233700600677)
XLA Ops:
  0.6 0.0 copy-start.9
  0.6 0.0 copy-start.10
  0.7 0.7 copy-done.9
  1.3 0.0 copy-done.10
  1.3 0.0 copy-start
  1.3 1.0 %copy-done = f32[1,2,3,8,2560]{4,3,2,1,0:T(8,128)S(1)} copy-done((f32[1,2,3,8,2560]{4,3,2,1,0:T(8,128)S(1)}, f32[1,2,3,8,2560]{4,3,2,1,0:T(8,128)}, u32[]{:S(2)}) %copy-start) | copy-done | bytes 491544
  2.4 0.0 copy-start.1
  2.4 1.0 %copy-done.1 = f32[20,40,128]{2,1,0:T(8,128)S(1)} copy-done((f32[20,40,128]{2,1,0:T(8,128)S(1)}, f32[20,40,128]{2,1,0:T(8,128)}, u32[]{:S(2)}) %copy-start.1) | copy-done | bytes 409624
  3.4 0.0 copy-start.2
  3.4 0.9 %copy-done.2 = f32[1,3,8,2560]{3,2,1,0:T(8,128)S(1)} copy-done((f32[1,3,8,2560]{3,2,1,0:T(8,128)S(1)}, f32[1,3,8,2560]{3,2,1,0:T(8,128)}, u32[]{:S(2)}) %copy-start.2) | copy-done | bytes 245784
  4.3 0.0 copy-start.3
  4.3 0.9 %copy-done.3 = bf16[384,256]{1,0:T(8,128)(2,1)S(1)} copy-done((bf16[384,256]{1,0:T(8,128)(2,1)S(1)}, bf16[384,256]{1,0:T(8,128)(2,1)}, u32[]{:S(2)}) %copy-start.3) | copy-done | bytes 196632
  5.2 0.0 copy-start.4
  5.2 0.9 %copy-done.4 = f32[8,40,40]{2,1,0:T(8,128)S(1)} copy-done((f32[8,40,40]{2,1,0:T(8,128)S(1)}, f32[8,40,40]{2,1,0:T(8,128)}, u32[]{:S(2)}) %copy-start.4) | copy-done | bytes 51224
  6.2 0.0 copy-start.5
  6.2 0.9 %copy-done.5 = bf16[384,128]{1,0:T(8,128)(2,1)S(1)} copy-done((bf16[384,128]{1,0:T(8,128)(2,1)S(1)}, bf16[384,128]{1,0:T(8,128)(2,1)}, u32[]{:S(2)}) %copy-start.5) | copy-done | bytes 98328
  7.1 0.0 copy-start.6
  7.1 0.8 copy-done.6
  7.9 0.0 copy-start.7
  7.9 0.8 copy-done.7
  8.7 0.8 copy-done.8
  9.4 73.2 %newton_step.1 = (f32[1,3,8,2560]{3,2,1,0:T(8,128)S(1)}, f32[1,3,8,2560]{3,2,1,0:T(8,128)S(1)}) custom-call(f32[1,3,8,2560]{3,2,1,0:T(8,128)S(1)} %copy-done.2, f32[1,2,3,8,2560]{4,3,2,1,0:T(8,128)S(1)} %copy-done, f32[320,40]{1,0:T(8,128)S(1)} %bitcast.1, s32[64,64]{1,0:T(8,128)S(1)} %copy-done.7, bf16[128,192]{1,0:T(8,128)(2,1)S(1)} %copy-done.6, ...), custom_call_target="tpu_custom_call" | custom-call | tf_op jit(solution)/shard_map/newton_step/pallas_call | solution.py:582
  82.7 0.7 copy.15
  83.4 0.7 copy.16
  (1 shorter events, 0.0 us)
Async XLA Ops:
  0.6 0.7 copy-start.9
  0.6 0.7 copy-start.10
  1.3 1.0 %copy-start = (f32[1,2,3,8,2560]{4,3,2,1,0:T(8,128)S(1)}, f32[1,2,3,8,2560]{4,3,2,1,0:T(8,128)}, u32[]{:S(2)}) copy-start(f32[1,2,3,8,2560]{4,3,2,1,0:T(8,128)} %panel.1) | copy-start | bytes 1474564
  2.4 1.0 %copy-start.1 = (f32[20,40,128]{2,1,0:T(8,128)S(1)}, f32[20,40,128]{2,1,0:T(8,128)}, u32[]{:S(2)}) copy-start(f32[20,40,128]{2,1,0:T(8,128)} %constant.18.clone.derivative_in) | copy-start | bytes 1228804
  3.4 0.9 %copy-start.2 = (f32[1,3,8,2560]{3,2,1,0:T(8,128)S(1)}, f32[1,3,8,2560]{3,2,1,0:T(8,128)}, u32[]{:S(2)}) copy-start(f32[1,3,8,2560]{3,2,1,0:T(8,128)} %states.1) | copy-start | bytes 737284
  4.3 0.9 %copy-start.3 = (bf16[384,256]{1,0:T(8,128)(2,1)S(1)}, bf16[384,256]{1,0:T(8,128)(2,1)}, u32[]{:S(2)}) copy-start(bf16[384,256]{1,0:T(8,128)(2,1)} %constant.16.clone.z_forward_in) | copy-start | bytes 589828
  5.2 0.9 %copy-start.4 = (f32[8,40,40]{2,1,0:T(8,128)S(1)}, f32[8,40,40]{2,1,0:T(8,128)}, u32[]{:S(2)}) copy-start(f32[8,40,40]{2,1,0:T(8,128)} %param.13) | copy-start | bytes 153604
  6.2 0.9 %copy-start.5 = (bf16[384,128]{1,0:T(8,128)(2,1)S(1)}, bf16[384,128]{1,0:T(8,128)(2,1)}, u32[]{:S(2)}) copy-start(bf16[384,128]{1,0:T(8,128)(2,1)} %constant.17.clone.z_back_in) | copy-start | bytes 294916
  7.1 0.8 copy-start.6
  7.9 0.8 copy-start.7
  8.7 0.8 copy-start.8

commit v2 on v1

--- a/solution.py
+++ b/solution.py
@@ -354,26 +354,28 @@
     keep = jnp.concatenate([own_rows, own_rows], axis=1) * damping[...]
 
     def transform(group):
-        def step(index, carry):
-            lanes = tile_at(index)
-
-            def modes(unit):
-                value = got[unit, group, :, :, :, lanes]
-                value = value.reshape(3, NX, TILE)
-                return stacked(jnp.concatenate([value[0], value[1], value[2]], axis=1), 0)
-
-            def by_rows(value):
-                return [value[:, c * TILE : (c + 1) * TILE] for c in range(3)]
-
-            in_x = mul(x_forward[...], modes(0))
-            in_x_wall = mul(x_forward[pl.ds(0, NX), :], modes(1))
-            plain = jnp.concatenate(by_rows(in_x[:NX]), axis=0)
-            rest = jnp.concatenate(by_rows(in_x[NX:]) + by_rows(in_x_wall), axis=0)
-            pair = mul(stacked(plain, 1), z_forward[...])
-            single = mul(stacked(rest, 1), z_forward[:, pl.ds(0, TILE)])
+        wait_heights(0, group)
+        wait_heights(1, group)
+
+        def modes(unit):
+            value = got[unit, group].reshape(3, NX, 3 * TILE)
+            return stacked(jnp.concatenate([value[0], value[1], value[2]], axis=1), 0)
+
+        def by_rows(value):
+            return [value[:, c * TILE : (c + 1) * TILE] for c in range(9)]
+
+        in_x = mul(x_forward[...], modes(0))
+        in_x_wall = mul(x_forward[pl.ds(0, NX), :], modes(1))
+        plain = jnp.concatenate(by_rows(in_x[:NX]), axis=0)
+        rest = jnp.concatenate(by_rows(in_x[NX:]) + by_rows(in_x_wall), axis=0)
+        pair = mul(stacked(plain, 1), z_forward[...])
+        single = mul(stacked(rest, 1), z_forward[:, pl.ds(0, TILE)])
+        total = [None] * 9
+        for index in range(3):
 
             def field(value, c):
-                return value[c * NX : (c + 1) * NX]
+                row = (3 * c + index) * NX
+                return value[row : row + NX]
 
             physical = [field(pair[:, :TILE], c) for c in range(3)]
             span = [field(pair[:, TILE:], c) for c in range(3)]
@@ -388,8 +390,7 @@
                 u, v, w = physical
             else:
                 u, v, w = (flow[index, c] for c in range(3))
-            u = u + heights[first_pair + index]
-            total = []
+            u = u + heights[lax.min(first_pair + index, PAIRS - 1)]
             for c in range(3):
                 value = u * stream[c] + v * slope[c] + w * span[c]
                 if group > 0:
@@ -400,33 +401,42 @@
                     )
                 if c == 0:
                     value += physical[1]
-                total.append(value)
-            in_k = mul(stacked(jnp.concatenate(total, axis=0), 1), z_back[...])
-            in_k = jnp.concatenate([field(in_k, c) for c in range(3)], axis=1)
-            in_m = mul(x_back[...], stacked(in_k, 0))
-            for c in range(3):
-                outgoing[group, index, c] = in_m[:, c * TILE : (c + 1) * TILE]
-            spot = tile_at(first_pair + index)
-            for hop in range(1, 8):
-                other = lax.rem(place + hop, 8)
+                total[3 * c + index] = value
+        in_k = mul(stacked(jnp.concatenate(total, axis=0), 1), z_back[...])
+        in_k = jnp.concatenate([in_k[c * NX : (c + 1) * NX] for c in range(9)], axis=1)
+        in_m = mul(x_back[...], stacked(in_k, 0))
+        for c in range(3):
+            outgoing[group, c] = in_m[:, 3 * c * TILE : 3 * (c + 1) * TILE]
+        for hop in range(1, 8):
+            other = lax.rem(place + hop, 8)
+            rows = pl.ds(pl.multiple_of(other * 8, 8), 8)
+
+            def send(start, tiles):
                 pltpu.make_async_remote_copy(
-                    src_ref=outgoing.at[
-                        group, index, :, pl.ds(pl.multiple_of(other * 8, 8), 8), :
-                    ],
-                    dst_ref=returned.at[group, :, :, spot],
+                    src_ref=outgoing.at[group, :, rows, pl.ds(start * TILE, tiles * TILE)],
+                    dst_ref=returned.at[group, :, :, tile_at(first_pair + start, tiles)],
                     send_sem=back_send.at[group],
                     recv_sem=back_recv.at[group],
                     device_id=(seg, other),
                     device_id_type=MESH,
                 ).start()
-            returned[group, :, :, spot] = outgoing[
-                group, index, :, pl.ds(pl.multiple_of(place * 8, 8), 8), :
+
+            send(0, 2)
+
+            @pl.when(count == 3)
+            def _():
+                send(2, 1)
+
+        own = pl.ds(pl.multiple_of(place * 8, 8), 8)
+        returned[group, :, :, tile_at(first_pair, 2)] = outgoing[
+            group, :, own, pl.ds(0, 2 * TILE)
+        ]
+
+        @pl.when(count == 3)
+        def _():
+            returned[group, :, :, tile_at(first_pair + 2)] = outgoing[
+                group, :, own, pl.ds(2 * TILE, TILE)
             ]
-            return carry
-
-        wait_heights(0, group)
-        wait_heights(1, group)
-        lax.fori_loop(0, count, step, 0)
 
     def finish(group):
         wait_pairs(back_recv.at[group])
@@ -527,11 +537,11 @@
     for group in range(3):
         @pl.when(count == 3)
         def _():
-            drain(outgoing.at[group, pl.ds(0, 3), :, pl.ds(0, 56), :], back_send.at[group])
+            drain(outgoing.at[group, :, pl.ds(0, 56), pl.ds(0, 3 * TILE)], back_send.at[group])
 
         @pl.when(count == 2)
         def _():
-            drain(outgoing.at[group, pl.ds(0, 2), :, pl.ds(0, 56), :], back_send.at[group])
+            drain(outgoing.at[group, :, pl.ds(0, 56), pl.ds(0, 2 * TILE)], back_send.at[group])
 
     for copy in shift:
         copy.wait_send()
@@ -560,7 +570,7 @@
         pltpu.VMEM(whole, f32),
         pltpu.VMEM((2, 3, 3, 8, 8, 3 * TILE), f32),
         pltpu.VMEM((3, 12, NX, TILE), f32),
-        pltpu.VMEM((3, 3, 3, NX, TILE), f32),
+        pltpu.VMEM((3, 3, NX, 3 * TILE), f32),
         pltpu.VMEM((3, 3, 8, LANES), f32),
         pltpu.VMEM((PAIRS, 2 * PAIRS, 8, TILE), f32),
         pltpu.VMEM(whole, f32),
@@ -586,7 +596,7 @@
         out_specs=[pl.BlockSpec(memory_space=pltpu.VMEM)] * 2,
         scratch_shapes=scratch,
         compiler_params=pltpu.CompilerParams(
-            collective_id=0, has_side_effects=True, vmem_limit_bytes=48 * 1024 * 1024
+            collective_id=0, has_side_effects=True, vmem_limit_bytes=64 * 1024 * 1024
         ),
         name="newton_step",
     )(*operands)

time: 84.6 us -> 76.8 us (0.908)
  local copies, waits for them, and re-layouts: 10.1 us -> 2.39 us
    unnamed x24 -> x4, local copies, waits for them, and re-layouts: 10.1 us -> 2.39 us
where the time goes in v2:
time: 76.8 us; the launch traced here: 76.6 us
  Pallas kernels  73.6 us (96%)
  local copies, waits for them, and re-layouts  2.39 us (3%)
    pallas_call x1, Pallas kernels, local(): pl.pallas_call(functools.partial(kernel, nseg), out_shape=[jax.ShapeDtype...  73.6 us
    unnamed x4, local copies, waits for them, and re-layouts  2.39 us

profile of v2, /device:TPU:1, one launch (start us, length us, event | category | flops | bytes accessed | tf_op | source)
XLA Modules:
  0.0 76.6 jit_solution(14120879709841245518)
XLA Ops:
  0.6 73.6 %newton_step.1 = (f32[1,3,8,2560]{3,2,1,0:T(8,128)}, f32[1,3,8,2560]{3,2,1,0:T(8,128)}) custom-call(f32[1,3,8,2560]{3,2,1,0:T(8,128)} %states.1, f32[1,2,3,8,2560]{4,3,2,1,0:T(8,128)} %panel.1, f32[320,40]{1,0:T(8,128)} %bitcast.1, s32[64,64]{1,0:T(8,128)} %mask.1, bf16[128,192]{1,0:T(8,128)(2,1)} %constant.14.clone.x_forward_in, ...), custom_call_target="tpu_custom_call" | custom-call | tf_op jit(solution)/shard_map/newton_step/pallas_call | solution.py:592
  74.2 0.0 copy-start
  74.2 1.7 %copy.15 = f32[1,3,8,2560]{3,2,1,0:T(8,128)} copy(f32[1,3,8,2560]{3,2,1,0:T(8,128)} %get-tuple-element.4) | data formatting | bytes 491520
  75.9 0.0 copy-done
  75.9 0.7 copy.16
Async XLA Ops:
  74.2 1.7 %copy-start = (f32[1,3,8,2560]{3,2,1,0:T(8,128)S(1)}, f32[1,3,8,2560]{3,2,1,0:T(8,128)}, u32[]{:S(2)}) copy-start(f32[1,3,8,2560]{3,2,1,0:T(8,128)} %get-tuple-element.5) | copy-start | bytes 737284

commit v3 on v2

--- a/solution.py
+++ b/solution.py
@@ -134,60 +134,85 @@
     damping,
     wall_v,
     mask_v,
+    home,
     fields,
     swapped,
     slopes,
     got,
+    passing,
     flow,
     outgoing,
+    passing_back,
     returned,
     solve,
     forced,
     turned,
     ends,
     later,
+    gaps,
+    gaps_home,
     near,
     far,
     in_sem,
+    trade_send,
+    trade_recv,
     out_send,
     out_recv,
+    pass_send,
+    pass_recv,
     back_send,
     back_recv,
+    pass_back_send,
+    pass_back_recv,
     later_send,
     later_recv,
+    home_send,
+    home_recv,
     sum_send,
     sum_recv,
 ):
     seg = lax.axis_index("seg")
-    place = lax.axis_index("space")
+    space = lax.axis_index("space")
     core = lax.rem(seg, 2)
+    side = lax.div(space, 4)
+    row = lax.rem(space, 4)
+    base = seg - core
     chip_pair = lax.div(seg, 2)
-    before = lax.rem(seg + nseg - 1, nseg)
-    across = lax.rem(seg + nseg + 2 * core - 1, nseg)
     near_count, far_count = 16, nseg // 2
-    near_me = core * 8 + place
+    near_me = core * 8 + space
+    place = core * 4 + row
+    traded = core + side == 1
+    trader = (base + side, place)
     first_pair, count = band(place)
 
     def near_device(step):
         other = lax.rem(near_me + step, near_count)
-        return (seg - core + lax.div(other, 8), lax.rem(other, 8))
+        return (base + lax.div(other, 8), lax.rem(other, 8))
 
     def far_device(step):
-        return (2 * lax.rem(chip_pair + step, far_count) + core, place)
+        return (2 * lax.rem(chip_pair + step, far_count) + core, space)
+
+    def member(kind, hop):
+        where = lax.rem(row + hop + 4, 4)
+        return kind * 4 + where, (base + kind, side * 4 + where)
+
+    next_pair = lax.rem(seg + 2 * side - 2 * (1 - side) + nseg, nseg)
+    across = (next_pair, space + 4 * (1 - side) - 4 * side)
 
     barrier = pltpu.get_barrier_semaphore()
     for step in range(1, near_count):
         pl.semaphore_signal(barrier, inc=1, device_id=near_device(step), device_id_type=MESH)
-    pl.semaphore_signal(barrier, inc=1, device_id=(across, place), device_id_type=MESH)
+    pl.semaphore_signal(barrier, inc=1, device_id=across, device_id_type=MESH)
     for step in range(1, far_count):
         pl.semaphore_signal(barrier, inc=1, device_id=far_device(step), device_id_type=MESH)
 
+    own = [states.at[0], panel.at[0, 0], panel.at[0, 1]]
+
+    def group_rows(group):
+        return pl.ds(3 * group, 3)
+
     loads = [
-        (states.at[0], fields.at[pl.ds(0, 3)]),
-        (panel.at[0, 0], fields.at[pl.ds(3, 3)]),
-        (panel.at[0, 1], fields.at[pl.ds(6, 3)]),
         (derivative_in, derivative),
-        (wall, wall_v),
         (mask, mask_v),
         (x_forward_in, x_forward),
         (z_forward_in, z_forward),
@@ -195,48 +220,115 @@
         (z_back_in, z_back),
         (heights_in, heights),
         (damping_in, damping),
+        *[(own[group], home.at[group_rows(group)]) for group in range(3)],
     ]
     loads = [
         pltpu.make_async_copy(src, dst, in_sem.at[index])
         for index, (src, dst) in enumerate(loads)
     ]
+    begins = [(own[group], fields.at[group_rows(group)]) for group in range(3)] + [(wall, wall_v)]
+
+    @pl.when(jnp.logical_not(traded))
+    def _():
+        for index, (src, dst) in enumerate(begins):
+            pltpu.make_async_copy(src, dst, trade_recv.at[index]).start()
+
     for load in loads:
         load.start()
     pl.semaphore_wait(barrier, near_count + far_count - 1)
 
+    def send(src, dst, send_sem, recv_sem, device):
+        pltpu.make_async_remote_copy(
+            src_ref=src,
+            dst_ref=dst,
+            send_sem=send_sem,
+            recv_sem=recv_sem,
+            device_id=device,
+            device_id_type=MESH,
+        ).start()
+
+    def send_tiles(src, dst, three, send_sem, recv_sem, device):
+        send(src(0, 2), dst(0, 2), send_sem, recv_sem, device)
+
+        @pl.when(three)
+        def _():
+            send(src(2, 1), dst(2, 1), send_sem, recv_sem, device)
+
+    @pl.when(traded)
+    def _():
+        for index, (src, dst) in enumerate(begins):
+            send(src, dst, trade_send.at[index], trade_recv.at[index], trader)
+
+    def slot(ref, *index):
+        return lambda start, tiles: ref.at[(*index, pl.ds(start * TILE, tiles * TILE))]
+
+    def band_of(ref, first, *index):
+        return lambda start, tiles: ref.at[(*index, tile_at(first + start, tiles))]
+
+    everything = slice(None)
+    direct = [(1 - core, 0), (0, 1), (1, 1), (0, 3), (1, 3)]
+    opposite = [(0, 1), (1, 3)]
+
     def send_heights(unit, group, source):
-        for step in range(1, 8):
-            other = lax.rem(place + step, 8)
+        sems = out_send.at[unit, group]
+        for way, (kind, hop) in enumerate(opposite):
+            other, _ = member(kind, 2)
+            _, relay = member(core, hop)
             other_first, other_count = band(other)
-            pltpu.make_async_remote_copy(
-                src_ref=source.at[:, :, tile_at(other_first, 2)],
-                dst_ref=got.at[unit, group, :, place, :, pl.ds(0, 2 * TILE)],
-                send_sem=out_send.at[unit, group],
-                recv_sem=out_recv.at[unit, group],
-                device_id=(seg, other),
-                device_id_type=MESH,
-            ).start()
-
-            @pl.when(other_count == 3)
-            def _():
-                pltpu.make_async_remote_copy(
-                    src_ref=source.at[:, :, tile_at(other_first + 2)],
-                    dst_ref=got.at[unit, group, :, place, :, pl.ds(2 * TILE, TILE)],
-                    send_sem=out_send.at[unit, group],
-                    recv_sem=out_recv.at[unit, group],
-                    device_id=(seg, other),
-                    device_id_type=MESH,
-                ).start()
+            send_tiles(
+                band_of(source, other_first, everything, everything),
+                slot(passing, unit, group, way, everything, everything),
+                other_count == 3,
+                sems,
+                pass_recv.at[unit, group, way],
+                relay,
+            )
+        for kind, hop in direct:
+            other, device = member(kind, hop)
+            other_first, other_count = band(other)
+            send_tiles(
+                band_of(source, other_first, everything, everything),
+                slot(got, unit, group, everything, place, everything),
+                other_count == 3,
+                sems,
+                out_recv.at[unit, group],
+                device,
+            )
+
+    def drain_tiles(ref, three, sem):
+        @pl.when(three)
+        def _():
+            drain(ref(0, 3), sem)
+
+        @pl.when(jnp.logical_not(three))
+        def _():
+            drain(ref(0, 2), sem)
+
+    def pass_heights(unit, group):
+        for way, (kind, hop) in enumerate(opposite):
+            origin, _ = member(core, hop + 2)
+            other, device = member(kind, hop)
+            _, other_count = band(other)
+            held = slot(passing, unit, group, way, everything, everything)
+            drain_tiles(held, other_count == 3, pass_recv.at[unit, group, way])
+            send_tiles(
+                held,
+                slot(got, unit, group, everything, origin, everything),
+                other_count == 3,
+                pass_send.at[unit, group, way],
+                out_recv.at[unit, group],
+                device,
+            )
 
     def keep_heights(unit, group, source):
         got[unit, group, :, place, :, pl.ds(0, 2 * TILE)] = source[
-            pl.ds(3 * group, 3), :, tile_at(first_pair, 2)
+            group_rows(group), :, tile_at(first_pair, 2)
         ]
 
         @pl.when(count == 3)
         def _():
             got[unit, group, :, place, :, pl.ds(2 * TILE, TILE)] = source[
-                pl.ds(3 * group, 3), :, tile_at(first_pair + 2)
+                group_rows(group), :, tile_at(first_pair + 2)
             ]
 
     def drain(ref, sem):
@@ -289,12 +381,12 @@
             lanes = pl.ds(pair * TILE, TILE)
             target[rows, :, lanes] = pltpu.roll(source[rows, :, lanes], NZ, 2)
 
-    for group in range(3):
-        source = states.at[0] if group == 0 else panel.at[0, group - 1]
-        send_heights(0, group, source)
-        loads[group].wait()
-        if group == 0:
-            loads[3].wait()
+    def begin(group):
+        drain(fields.at[group_rows(group)], trade_recv.at[group])
+        send_heights(0, group, fields.at[group_rows(group)])
+        keep_heights(0, group, fields)
+
+    def differentiate(group):
         turn(group, fields, swapped)
         across_heights(
             group,
@@ -303,31 +395,42 @@
             lambda pair, row: derivative[pair, pl.ds(row, 1), :],
             slopes,
         )
-        send_heights(1, group, slopes.at[pl.ds(3 * group, 3)])
-        keep_heights(0, group, fields)
+
+    def send_slopes(group):
+        send_heights(1, group, slopes.at[group_rows(group)])
         keep_heights(1, group, slopes)
 
-    shift = [
-        pltpu.make_async_remote_copy(
-            src_ref=src,
-            dst_ref=dst,
-            send_sem=later_send.at[index],
-            recv_sem=later_recv.at[index],
-            device_id=(before, place),
-            device_id_type=MESH,
-        )
-        for index, (src, dst) in enumerate(
-            [
-                (states.at[0], later.at[pl.ds(0, 3)]),
-                (panel.at[0, 0], later.at[pl.ds(3, 3)]),
-                (panel.at[0, 1], later.at[pl.ds(6, 3)]),
-            ]
-        )
-    ]
-    for copy in shift:
-        copy.start()
-    for load in loads[4:]:
-        load.wait()
+    def send_start(sources, device):
+        for group in range(3):
+            send(
+                sources[group],
+                later.at[group_rows(group)],
+                later_send.at[group],
+                later_recv.at[group],
+                device,
+            )
+
+    def shift():
+        mine = [fields.at[group_rows(group)] for group in range(3)]
+
+        @pl.when(side == 0)
+        def _():
+            send_start(mine, across)
+
+        @pl.when(core * side == 1)
+        def _():
+            send_start(mine, (seg, space - 4))
+
+        @pl.when(core * (1 - side) == 1)
+        def _():
+            for group in range(3):
+                send(
+                    own[group],
+                    later.at[group_rows(group)],
+                    home_send.at[3 + group],
+                    later_recv.at[group],
+                    (seg - 1, space),
+                )
 
     lane = lax.broadcasted_iota(jnp.int32, (8, TILE), 1)
     low_half = lane < NZ
@@ -348,10 +451,9 @@
             )
         return carry
 
-    lax.fori_loop(0, PAIRS, solve_rows, 0)
-
-    own_rows = mask_v[pl.ds(pl.multiple_of(place * 8, 8), 8), :].astype(jnp.float32)
-    keep = jnp.concatenate([own_rows, own_rows], axis=1) * damping[...]
+    def kept():
+        rows = mask_v[pl.ds(pl.multiple_of(place * 8, 8), 8), :].astype(jnp.float32)
+        return jnp.concatenate([rows, rows], axis=1) * damping[...]
 
     def transform(group):
         wait_heights(0, group)
@@ -407,40 +509,62 @@
         in_m = mul(x_back[...], stacked(in_k, 0))
         for c in range(3):
             outgoing[group, c] = in_m[:, 3 * c * TILE : 3 * (c + 1) * TILE]
-        for hop in range(1, 8):
-            other = lax.rem(place + hop, 8)
-            rows = pl.ds(pl.multiple_of(other * 8, 8), 8)
-
-            def send(start, tiles):
-                pltpu.make_async_remote_copy(
-                    src_ref=outgoing.at[group, :, rows, pl.ds(start * TILE, tiles * TILE)],
-                    dst_ref=returned.at[group, :, :, tile_at(first_pair + start, tiles)],
-                    send_sem=back_send.at[group],
-                    recv_sem=back_recv.at[group],
-                    device_id=(seg, other),
-                    device_id_type=MESH,
-                ).start()
-
-            send(0, 2)
-
-            @pl.when(count == 3)
-            def _():
-                send(2, 1)
-
-        own = pl.ds(pl.multiple_of(place * 8, 8), 8)
+
+        def rows_of(other):
+            return pl.ds(pl.multiple_of(other * 8, 8), 8)
+
+        for way, (kind, hop) in enumerate(opposite):
+            other, _ = member(kind, 2)
+            _, relay = member(core, hop)
+            send_tiles(
+                slot(outgoing, group, everything, rows_of(other)),
+                slot(passing_back, group, way, everything, everything),
+                count == 3,
+                back_send.at[group],
+                pass_back_recv.at[group, way],
+                relay,
+            )
+        for kind, hop in direct:
+            other, device = member(kind, hop)
+            send_tiles(
+                slot(outgoing, group, everything, rows_of(other)),
+                band_of(returned, first_pair, group, everything, everything),
+                count == 3,
+                back_send.at[group],
+                back_recv.at[group],
+                device,
+            )
+
+        mine = rows_of(place)
         returned[group, :, :, tile_at(first_pair, 2)] = outgoing[
-            group, :, own, pl.ds(0, 2 * TILE)
+            group, :, mine, pl.ds(0, 2 * TILE)
         ]
 
         @pl.when(count == 3)
         def _():
             returned[group, :, :, tile_at(first_pair + 2)] = outgoing[
-                group, :, own, pl.ds(2 * TILE, TILE)
+                group, :, mine, pl.ds(2 * TILE, TILE)
             ]
 
-    def finish(group):
+    def pass_back(group):
+        for way, (kind, hop) in enumerate(opposite):
+            origin, _ = member(core, hop + 2)
+            _, device = member(kind, hop)
+            origin_first, origin_count = band(origin)
+            held = slot(passing_back, group, way, everything, everything)
+            drain_tiles(held, origin_count == 3, pass_back_recv.at[group, way])
+            send_tiles(
+                held,
+                band_of(returned, origin_first, group, everything, everything),
+                origin_count == 3,
+                pass_back_send.at[group, way],
+                back_recv.at[group],
+                device,
+            )
+
+    def finish(group, keep):
         wait_pairs(back_recv.at[group])
-        rows = pl.ds(3 * group, 3)
+        rows = group_rows(group)
         for pair in range(PAIRS):
             lanes = pl.ds(pair * TILE, TILE)
             value = keep * (fields[rows, :, lanes] + returned[group, :, :, lanes])
@@ -449,24 +573,61 @@
         across_heights(
             group, forced, turned, lambda pair, row: solve[pair, row], ends
         )
-
+        drain(later.at[rows], later_recv.at[group])
+        gap = ends[rows] - later[rows]
+        gaps[rows] = gap
+
+        @pl.when(traded)
+        def _():
+            send(
+                gaps.at[rows],
+                gaps_home.at[rows],
+                home_send.at[group],
+                home_recv.at[group],
+                trader,
+            )
+
+        @pl.when(jnp.logical_not(traded))
+        def _():
+            gaps_home[rows] = gap
+
+    begin(0)
+    loads[0].wait()
+    differentiate(0)
+    send_slopes(0)
+    pass_heights(0, 0)
+    begin(1)
+    differentiate(1)
+    pass_heights(1, 0)
+    send_slopes(1)
+    drain(wall_v, trade_recv.at[3])
+    lax.fori_loop(0, PAIRS, solve_rows, 0)
+    pass_heights(0, 1)
+    begin(2)
+    differentiate(2)
+    pass_heights(1, 1)
+    send_slopes(2)
+    shift()
+    for load in loads[1:]:
+        load.wait()
+    keep = kept()
+    pass_heights(0, 2)
     transform(0)
+    pass_heights(1, 2)
     transform(1)
-    finish(0)
+    pass_back(0)
     transform(2)
-    finish(1)
-    for copy in shift:
-        copy.wait_recv()
-    finish(2)
+    pass_back(1)
+    finish(0, keep)
+    pass_back(2)
+    finish(1, keep)
+    finish(2, keep)
 
     def products(index, sums):
         lanes = tile_at(index)
-        start = [fields[pl.ds(3 * g, 3), :, lanes] for g in range(3)]
-        end = [ends[pl.ds(3 * g, 3), :, lanes] for g in range(3)]
-        gap = [end[g] - later[pl.ds(3 * g, 3), :, lanes] for g in range(3)]
-        for g in range(3):
-            ends[pl.ds(3 * g, 3), :, lanes] = gap[g]
-        drift = end[0] - start[0]
+        start = [fields[group_rows(g), :, lanes] for g in range(3)]
+        gap = [gaps[group_rows(g), :, lanes] for g in range(3)]
+        drift = ends[group_rows(0), :, lanes] - start[0]
         terms = [
             drift * start[1],
             drift * start[2],
@@ -481,11 +642,11 @@
     sums = lax.fori_loop(
         0, PAIRS, products, tuple(jnp.zeros((8, TILE), jnp.float32) for _ in range(7))
     )
-    row = lax.broadcasted_iota(jnp.int32, (1, TILE), 1)
+    column = lax.broadcasted_iota(jnp.int32, (1, TILE), 1)
     message = jnp.zeros((1, TILE), jnp.float32)
     for index, value in enumerate(sums):
         total = jnp.sum(jnp.sum(value, axis=0, keepdims=True), axis=1, keepdims=True)
-        message = jnp.where(row == index, total, message)
+        message = jnp.where(column == index, total, message)
 
     def exchange(which, slots, me, size, device, value):
         slots[me] = value
@@ -519,9 +680,14 @@
     ]
     weight = [jnp.broadcast_to(value, (8, TILE)) for value in weight]
 
+    @pl.when(traded)
+    def _():
+        for group in range(3):
+            drain(gaps_home.at[group_rows(group)], home_recv.at[group])
+
     def write(index, carry):
         lanes = tile_at(index)
-        for source, target in ((fields, corrected), (ends, new_residual)):
+        for source, target in ((home, corrected), (gaps_home, new_residual)):
             target[0, :, :, lanes] = (
                 source[pl.ds(0, 3), :, lanes]
                 + weight[0] * source[pl.ds(3, 3), :, lanes]
@@ -543,8 +709,41 @@
         def _():
             drain(outgoing.at[group, :, pl.ds(0, 56), pl.ds(0, 2 * TILE)], back_send.at[group])
 
-    for copy in shift:
-        copy.wait_send()
+    for group in range(3):
+        for way, (kind, hop) in enumerate(opposite):
+            other, _ = member(kind, hop)
+            _, other_count = band(other)
+            origin, _ = member(core, hop + 2)
+            _, origin_count = band(origin)
+            for unit in range(2):
+                drain_tiles(
+                    slot(passing, unit, group, way, everything, everything),
+                    other_count == 3,
+                    pass_send.at[unit, group, way],
+                )
+            drain_tiles(
+                slot(passing_back, group, way, everything, everything),
+                origin_count == 3,
+                pass_back_send.at[group, way],
+            )
+
+    @pl.when(traded)
+    def _():
+        for group in range(3):
+            drain(fields.at[group_rows(group)], trade_send.at[group])
+            drain(gaps.at[group_rows(group)], home_send.at[group])
+        drain(wall_v, trade_send.at[3])
+
+    @pl.when(jnp.logical_or(side == 0, core * side == 1))
+    def _():
+        for group in range(3):
+            drain(fields.at[group_rows(group)], later_send.at[group])
+
+    @pl.when(core * (1 - side) == 1)
+    def _():
+        for group in range(3):
+            drain(home.at[group_rows(group)], home_send.at[3 + group])
+
     drain(near.at[pl.ds(0, near_count - 1)], sum_send.at[0])
     if far_count > 1:
         drain(far.at[pl.ds(0, far_count - 1)], sum_send.at[1])
@@ -565,26 +764,31 @@
         *[pltpu.VMEM(value.shape, value.dtype) for value in constants],
         pltpu.VMEM((8 * NY, NY), f32),
         pltpu.VMEM((NX, NZ), jnp.int32),
-        pltpu.VMEM(whole, f32),
-        pltpu.VMEM(whole, f32),
-        pltpu.VMEM(whole, f32),
+        *[pltpu.VMEM(whole, f32)] * 4,
         pltpu.VMEM((2, 3, 3, 8, 8, 3 * TILE), f32),
+        pltpu.VMEM((2, 3, 2, 3, 8, 3 * TILE), f32),
         pltpu.VMEM((3, 12, NX, TILE), f32),
         pltpu.VMEM((3, 3, NX, 3 * TILE), f32),
+        pltpu.VMEM((3, 2, 3, 8, 3 * TILE), f32),
         pltpu.VMEM((3, 3, 8, LANES), f32),
         pltpu.VMEM((PAIRS, 2 * PAIRS, 8, TILE), f32),
-        pltpu.VMEM(whole, f32),
-        pltpu.VMEM(whole, f32),
-        pltpu.VMEM(whole, f32),
-        pltpu.VMEM(whole, f32),
+        *[pltpu.VMEM(whole, f32)] * 6,
         pltpu.VMEM((16, 1, TILE), f32),
         pltpu.VMEM((nseg // 2, 1, TILE), f32),
-        sem((12,)),
+        sem((11,)),
+        sem((4,)),
+        sem((4,)),
         sem((2, 3)),
         sem((2, 3)),
+        sem((2, 3, 2)),
+        sem((2, 3, 2)),
         sem((3,)),
         sem((3,)),
+        sem((3, 2)),
+        sem((3, 2)),
         sem((3,)),
+        sem((3,)),
+        sem((6,)),
         sem((3,)),
         sem((2,)),
         sem((2,)),

time: 76.8 us -> 73.5 us (0.957)
  Pallas kernels: 73.6 us -> 70.1 us
    pallas_call x1, Pallas kernels: 73.6 us -> 70.1 us  [local(): pl.pallas_call(functools.partial(kernel, nseg), out_shape=[jax.ShapeDtype...]
where the time goes in v3:
time: 73.5 us; the launch traced here: 73.2 us
  Pallas kernels  70.1 us (95%)
  local copies, waits for them, and re-layouts  2.39 us (3%)
    pallas_call x1, Pallas kernels, local(): pl.pallas_call(functools.partial(kernel, nseg), out_shape=[jax.ShapeDtype...  70.1 us
    unnamed x4, local copies, waits for them, and re-layouts  2.39 us

profile of v3, /device:TPU:1, one launch (start us, length us, event | category | flops | bytes accessed | tf_op | source)
XLA Modules:
  0.0 73.2 jit_solution(16947936421457421031)
XLA Ops:
  0.6 70.1 %newton_step.1 = (f32[1,3,8,2560]{3,2,1,0:T(8,128)}, f32[1,3,8,2560]{3,2,1,0:T(8,128)}) custom-call(f32[1,3,8,2560]{3,2,1,0:T(8,128)} %states.1, f32[1,2,3,8,2560]{4,3,2,1,0:T(8,128)} %panel.1, f32[320,40]{1,0:T(8,128)} %bitcast.1, s32[64,64]{1,0:T(8,128)} %mask.1, bf16[128,192]{1,0:T(8,128)(2,1)} %constant.14.clone.x_forward_in, ...), custom_call_target="tpu_custom_call" | custom-call | tf_op jit(solution)/shard_map/newton_step/pallas_call | solution.py:796
  70.8 0.0 copy-start
  70.8 1.7 %copy.15 = f32[1,3,8,2560]{3,2,1,0:T(8,128)} copy(f32[1,3,8,2560]{3,2,1,0:T(8,128)} %get-tuple-element.4) | data formatting | bytes 491520
  72.5 0.0 copy-done
  72.5 0.7 copy.16
Async XLA Ops:
  70.8 1.7 %copy-start = (f32[1,3,8,2560]{3,2,1,0:T(8,128)S(1)}, f32[1,3,8,2560]{3,2,1,0:T(8,128)}, u32[]{:S(2)}) copy-start(f32[1,3,8,2560]{3,2,1,0:T(8,128)} %get-tuple-element.5) | copy-start | bytes 737284

commit v4 on v3

--- a/solution.py
+++ b/solution.py
@@ -123,8 +123,8 @@
     derivative_in,
     heights_in,
     damping_in,
-    corrected,
-    new_residual,
+    gaps_home,
+    message_out,
     x_forward,
     x_back,
     z_forward,
@@ -134,7 +134,6 @@
     damping,
     wall_v,
     mask_v,
-    home,
     fields,
     swapped,
     slopes,
@@ -150,9 +149,6 @@
     ends,
     later,
     gaps,
-    gaps_home,
-    near,
-    far,
     in_sem,
     trade_send,
     trade_recv,
@@ -168,8 +164,6 @@
     later_recv,
     home_send,
     home_recv,
-    sum_send,
-    sum_recv,
 ):
     seg = lax.axis_index("seg")
     space = lax.axis_index("space")
@@ -177,8 +171,7 @@
     side = lax.div(space, 4)
     row = lax.rem(space, 4)
     base = seg - core
-    chip_pair = lax.div(seg, 2)
-    near_count, far_count = 16, nseg // 2
+    near_count = 16
     near_me = core * 8 + space
     place = core * 4 + row
     traded = core + side == 1
@@ -189,9 +182,6 @@
         other = lax.rem(near_me + step, near_count)
         return (base + lax.div(other, 8), lax.rem(other, 8))
 
-    def far_device(step):
-        return (2 * lax.rem(chip_pair + step, far_count) + core, space)
-
     def member(kind, hop):
         where = lax.rem(row + hop + 4, 4)
         return kind * 4 + where, (base + kind, side * 4 + where)
@@ -203,8 +193,6 @@
     for step in range(1, near_count):
         pl.semaphore_signal(barrier, inc=1, device_id=near_device(step), device_id_type=MESH)
     pl.semaphore_signal(barrier, inc=1, device_id=across, device_id_type=MESH)
-    for step in range(1, far_count):
-        pl.semaphore_signal(barrier, inc=1, device_id=far_device(step), device_id_type=MESH)
 
     own = [states.at[0], panel.at[0, 0], panel.at[0, 1]]
 
@@ -220,13 +208,12 @@
         (z_back_in, z_back),
         (heights_in, heights),
         (damping_in, damping),
-        *[(own[group], home.at[group_rows(group)]) for group in range(3)],
     ]
     loads = [
         pltpu.make_async_copy(src, dst, in_sem.at[index])
         for index, (src, dst) in enumerate(loads)
     ]
-    begins = [(own[group], fields.at[group_rows(group)]) for group in range(3)] + [(wall, wall_v)]
+    begins = [(wall, wall_v)] + [(own[group], fields.at[group_rows(group)]) for group in range(3)]
 
     @pl.when(jnp.logical_not(traded))
     def _():
@@ -235,7 +222,7 @@
 
     for load in loads:
         load.start()
-    pl.semaphore_wait(barrier, near_count + far_count - 1)
+    pl.semaphore_wait(barrier, near_count)
 
     def send(src, dst, send_sem, recv_sem, device):
         pltpu.make_async_remote_copy(
@@ -382,7 +369,7 @@
             target[rows, :, lanes] = pltpu.roll(source[rows, :, lanes], NZ, 2)
 
     def begin(group):
-        drain(fields.at[group_rows(group)], trade_recv.at[group])
+        drain(fields.at[group_rows(group)], trade_recv.at[1 + group])
         send_heights(0, group, fields.at[group_rows(group)])
         keep_heights(0, group, fields)
 
@@ -591,6 +578,8 @@
         def _():
             gaps_home[rows] = gap
 
+    drain(wall_v, trade_recv.at[0])
+    lax.fori_loop(0, PAIRS, solve_rows, 0)
     begin(0)
     loads[0].wait()
     differentiate(0)
@@ -600,8 +589,6 @@
     differentiate(1)
     pass_heights(1, 0)
     send_slopes(1)
-    drain(wall_v, trade_recv.at[3])
-    lax.fori_loop(0, PAIRS, solve_rows, 0)
     pass_heights(0, 1)
     begin(2)
     differentiate(2)
@@ -648,54 +635,12 @@
         total = jnp.sum(jnp.sum(value, axis=0, keepdims=True), axis=1, keepdims=True)
         message = jnp.where(column == index, total, message)
 
-    def exchange(which, slots, me, size, device, value):
-        slots[me] = value
-        for step in range(1, size):
-            pltpu.make_async_remote_copy(
-                src_ref=slots.at[me],
-                dst_ref=slots.at[me],
-                send_sem=sum_send.at[which],
-                recv_sem=sum_recv.at[which],
-                device_id=device(step),
-                device_id_type=MESH,
-            ).start()
-        if size > 1:
-            drain(slots.at[pl.ds(0, size - 1)], sum_recv.at[which])
-        return jnp.sum(slots[...], axis=0)
-
-    message = exchange(0, near, near_me, near_count, near_device, message)
-    message = exchange(1, far, chip_pair, far_count, far_device, message)
-
-    def number(index):
-        return message[:, index : index + 1]
-
-    root = 1.0 / math.sqrt(nseg * 3 * NX * LANES)
-    border = [number(0) * root, number(1) * root]
-    diag = [number(2) + border[0] * border[0], number(3) + border[1] * border[1]]
-    first = [-number(4) / diag[0], -number(5) / diag[1]]
-    cross = number(6) + border[0] * border[1]
-    weight = [
-        first[0] - first[1] * cross / diag[0],
-        first[1] - first[0] * cross / diag[1],
-    ]
-    weight = [jnp.broadcast_to(value, (8, TILE)) for value in weight]
+    message_out[...] = message
 
     @pl.when(traded)
     def _():
         for group in range(3):
             drain(gaps_home.at[group_rows(group)], home_recv.at[group])
-
-    def write(index, carry):
-        lanes = tile_at(index)
-        for source, target in ((home, corrected), (gaps_home, new_residual)):
-            target[0, :, :, lanes] = (
-                source[pl.ds(0, 3), :, lanes]
-                + weight[0] * source[pl.ds(3, 3), :, lanes]
-                + weight[1] * source[pl.ds(6, 3), :, lanes]
-            )
-        return carry
-
-    lax.fori_loop(0, PAIRS, write, 0)
 
     for unit in range(2):
         for group in range(3):
@@ -730,9 +675,9 @@
     @pl.when(traded)
     def _():
         for group in range(3):
-            drain(fields.at[group_rows(group)], trade_send.at[group])
+            drain(fields.at[group_rows(group)], trade_send.at[1 + group])
             drain(gaps.at[group_rows(group)], home_send.at[group])
-        drain(wall_v, trade_send.at[3])
+        drain(wall_v, trade_send.at[0])
 
     @pl.when(jnp.logical_or(side == 0, core * side == 1))
     def _():
@@ -742,11 +687,80 @@
     @pl.when(core * (1 - side) == 1)
     def _():
         for group in range(3):
-            drain(home.at[group_rows(group)], home_send.at[3 + group])
-
+            drain(fields.at[group_rows(group)], home_send.at[3 + group])
+
+
+def sum_kernel(nseg, message, weights, near, far, sum_send, sum_recv):
+    seg = lax.axis_index("seg")
+    space = lax.axis_index("space")
+    core = lax.rem(seg, 2)
+    chip_pair = lax.div(seg, 2)
+    near_count, far_count = 16, nseg // 2
+    near_me = core * 8 + space
+
+    def near_device(step):
+        other = lax.rem(near_me + step, near_count)
+        return (seg - core + lax.div(other, 8), lax.rem(other, 8))
+
+    def far_device(step):
+        return (2 * lax.rem(chip_pair + step, far_count) + core, space)
+
+    barrier = pltpu.get_barrier_semaphore()
+    for step in range(1, near_count):
+        pl.semaphore_signal(barrier, inc=1, device_id=near_device(step), device_id_type=MESH)
+    for step in range(1, far_count):
+        pl.semaphore_signal(barrier, inc=1, device_id=far_device(step), device_id_type=MESH)
+    pl.semaphore_wait(barrier, near_count + far_count - 2)
+
+    def drain(ref, sem):
+        pltpu.make_async_copy(ref, ref, sem).wait()
+
+    def exchange(which, slots, me, size, device, value):
+        slots[me] = value
+        for step in range(1, size):
+            pltpu.make_async_remote_copy(
+                src_ref=slots.at[me],
+                dst_ref=slots.at[me],
+                send_sem=sum_send.at[which],
+                recv_sem=sum_recv.at[which],
+                device_id=device(step),
+                device_id_type=MESH,
+            ).start()
+        if size > 1:
+            drain(slots.at[pl.ds(0, size - 1)], sum_recv.at[which])
+        return jnp.sum(slots[...], axis=0)
+
+    total = exchange(0, near, near_me, near_count, near_device, message[...])
+    total = exchange(1, far, chip_pair, far_count, far_device, total)
+
+    def number(index):
+        return total[:, index : index + 1]
+
+    root = 1.0 / math.sqrt(nseg * 3 * NX * LANES)
+    border = [number(0) * root, number(1) * root]
+    diag = [number(2) + border[0] * border[0], number(3) + border[1] * border[1]]
+    first = [-number(4) / diag[0], -number(5) / diag[1]]
+    cross = number(6) + border[0] * border[1]
+    weights[pl.ds(0, 1), :] = jnp.broadcast_to(first[0] - first[1] * cross / diag[0], (1, TILE))
+    weights[pl.ds(1, 1), :] = jnp.broadcast_to(first[1] - first[0] * cross / diag[1], (1, TILE))
     drain(near.at[pl.ds(0, near_count - 1)], sum_send.at[0])
     if far_count > 1:
         drain(far.at[pl.ds(0, far_count - 1)], sum_send.at[1])
+
+
+def final_kernel(states, panel, gaps, weights, corrected, new_residual):
+    a = jnp.broadcast_to(weights[pl.ds(0, 1), :], (8, TILE))
+    b = jnp.broadcast_to(weights[pl.ds(1, 1), :], (8, TILE))
+    for pair in range(PAIRS):
+        lanes = pl.ds(pair * TILE, TILE)
+        corrected[0, :, :, lanes] = (
+            states[0, :, :, lanes] + a * panel[0, 0, :, :, lanes] + b * panel[0, 1, :, :, lanes]
+        )
+        new_residual[0, :, :, lanes] = (
+            gaps[pl.ds(0, 3), :, lanes]
+            + a * gaps[pl.ds(3, 3), :, lanes]
+            + b * gaps[pl.ds(6, 3), :, lanes]
+        )
 
 
 def local(nseg, constants, states, tangent_panel, wall_inverse, keep_mask):
@@ -764,7 +778,7 @@
         *[pltpu.VMEM(value.shape, value.dtype) for value in constants],
         pltpu.VMEM((8 * NY, NY), f32),
         pltpu.VMEM((NX, NZ), jnp.int32),
-        *[pltpu.VMEM(whole, f32)] * 4,
+        *[pltpu.VMEM(whole, f32)] * 3,
         pltpu.VMEM((2, 3, 3, 8, 8, 3 * TILE), f32),
         pltpu.VMEM((2, 3, 2, 3, 8, 3 * TILE), f32),
         pltpu.VMEM((3, 12, NX, TILE), f32),
@@ -772,10 +786,8 @@
         pltpu.VMEM((3, 2, 3, 8, 3 * TILE), f32),
         pltpu.VMEM((3, 3, 8, LANES), f32),
         pltpu.VMEM((PAIRS, 2 * PAIRS, 8, TILE), f32),
-        *[pltpu.VMEM(whole, f32)] * 6,
-        pltpu.VMEM((16, 1, TILE), f32),
-        pltpu.VMEM((nseg // 2, 1, TILE), f32),
-        sem((11,)),
+        *[pltpu.VMEM(whole, f32)] * 5,
+        sem((8,)),
         sem((4,)),
         sem((4,)),
         sem((2, 3)),
@@ -790,20 +802,47 @@
         sem((3,)),
         sem((6,)),
         sem((3,)),
-        sem((2,)),
-        sem((2,)),
     ]
-    return pl.pallas_call(
+    vmem = pl.BlockSpec(memory_space=pltpu.VMEM)
+    gaps, message = pl.pallas_call(
         functools.partial(kernel, nseg),
-        out_shape=[jax.ShapeDtypeStruct((1, 3, 8, LANES), f32)] * 2,
+        out_shape=[
+            jax.ShapeDtypeStruct(whole, f32),
+            jax.ShapeDtypeStruct((1, TILE), f32),
+        ],
         in_specs=[pl.BlockSpec(memory_space=pl.ANY)] * len(operands),
-        out_specs=[pl.BlockSpec(memory_space=pltpu.VMEM)] * 2,
+        out_specs=[vmem, vmem],
         scratch_shapes=scratch,
         compiler_params=pltpu.CompilerParams(
             collective_id=0, has_side_effects=True, vmem_limit_bytes=64 * 1024 * 1024
         ),
         name="newton_step",
     )(*operands)
+    weights = pl.pallas_call(
+        functools.partial(sum_kernel, nseg),
+        out_shape=jax.ShapeDtypeStruct((2, TILE), f32),
+        in_specs=[vmem],
+        out_specs=vmem,
+        scratch_shapes=[
+            pltpu.VMEM((16, 1, TILE), f32),
+            pltpu.VMEM((nseg // 2, 1, TILE), f32),
+            sem((2,)),
+            sem((2,)),
+        ],
+        compiler_params=pltpu.CompilerParams(
+            collective_id=1, has_side_effects=True, vmem_limit_bytes=64 * 1024 * 1024
+        ),
+        name="newton_sums",
+    )(message)
+    result = jax.ShapeDtypeStruct((1, 3, 8, LANES), f32)
+    return pl.pallas_call(
+        final_kernel,
+        out_shape=[result, result],
+        in_specs=[vmem] * 4,
+        out_specs=[vmem, vmem],
+        compiler_params=pltpu.CompilerParams(vmem_limit_bytes=64 * 1024 * 1024),
+        name="newton_final",
+    )(states, tangent_panel, gaps, weights)
 
 
 def solution(mesh):

time: 73.5 us -> 78.7 us (1.071)
  Pallas kernels: 70.1 us -> 77.9 us
  local copies, waits for them, and re-layouts: 2.39 us -> 0 us
    pallas_call x0 -> x2, Pallas kernels: none -> 21.6 us  [the longest x1 19.4 us: local(): pl.pallas_call(functools.partial(sum_kernel, nseg), out_shape=jax.ShapeDt...]
    pallas_call x1, Pallas kernels: 70.1 us -> 56.3 us  [local(): pl.pallas_call(functools.partial(kernel, nseg), out_shape=[jax.ShapeDtype...]
    unnamed x4 -> x0, local copies, waits for them, and re-layouts: 2.39 us -> none
where the time goes in v4:
time: 78.7 us; the launch traced here: 78.6 us
  Pallas kernels  77.9 us (99%)
    pallas_call x1, Pallas kernels, local(): pl.pallas_call(functools.partial(kernel, nseg), out_shape=[jax.ShapeDtype...  56.3 us
    pallas_call x1, Pallas kernels, local(): pl.pallas_call(functools.partial(sum_kernel, nseg), out_shape=jax.ShapeDt...  19.4 us
    pallas_call x1, Pallas kernels, local(): pl.pallas_call(final_kernel, out_shape=[result, result], in_specs=[vmem]...  2.23 us

profile of v4, /device:TPU:1, one launch (start us, length us, event | category | flops | bytes accessed | tf_op | source)
XLA Modules:
  0.0 78.6 jit_solution(7614062671789602309)
XLA Ops:
  0.6 56.3 %newton_step.1 = (f32[9,8,2560]{2,1,0:T(8,128)}, f32[1,128]{1,0:T(1,128)}) custom-call(f32[1,3,8,2560]{3,2,1,0:T(8,128)} %states.3, f32[1,2,3,8,2560]{4,3,2,1,0:T(8,128)} %panel.3, f32[320,40]{1,0:T(8,128)} %bitcast.1, s32[64,64]{1,0:T(8,128)} %mask.1, bf16[128,192]{1,0:T(8,128)(2,1)} %constant.14.clone.x_forward_in, ...), custom_call_target="tpu_custom_call" | custom-call | tf_op jit(solution)/shard_map/newton_step/pallas_call | solution.py:807
  56.9 19.4 %newton_sums.1.weights = f32[2,128]{1,0:T(2,128)} custom-call(f32[1,128]{1,0:T(1,128)} %get-tuple-element.5.message), custom_call_target="tpu_custom_call" | custom-call | tf_op jit(solution)/shard_map/newton_sums/pallas_call | solution.py:821
  76.3 2.2 %newton_final.1 = (f32[1,3,8,2560]{3,2,1,0:T(8,128)}, f32[1,3,8,2560]{3,2,1,0:T(8,128)}) custom-call(f32[1,3,8,2560]{3,2,1,0:T(8,128)} %states.3, f32[1,2,3,8,2560]{4,3,2,1,0:T(8,128)} %panel.3, f32[9,8,2560]{2,1,0:T(8,128)} %get-tuple-element.4.gaps, f32[2,128]{1,0:T(2,128)} %newton_sums.1.weights), custom_call_target="tpu_custom_call" | custom-call | tf_op jit(solution)/shard_map/newton_final/pallas_call | solution.py:838

commit v5 on v3

--- a/solution.py
+++ b/solution.py
@@ -135,9 +135,8 @@
     wall_v,
     mask_v,
     home,
-    fields,
+    pack,
     swapped,
-    slopes,
     got,
     passing,
     flow,
@@ -151,8 +150,9 @@
     later,
     gaps,
     gaps_home,
-    near,
-    far,
+    ring_sums,
+    side_sums,
+    far_sums,
     in_sem,
     trade_send,
     trade_recv,
@@ -178,20 +178,17 @@
     row = lax.rem(space, 4)
     base = seg - core
     chip_pair = lax.div(seg, 2)
-    near_count, far_count = 16, nseg // 2
-    near_me = core * 8 + space
+    low_count = min(4, nseg // 2)
+    far_count = nseg // 2 // low_count
+    side_count = 2 * low_count
+    low, high = lax.rem(chip_pair, low_count), lax.div(chip_pair, low_count)
+    side_me = side * low_count + low
+    fields, slopes = pack.at[0], pack.at[1]
     place = core * 4 + row
     traded = core + side == 1
     trader = (base + side, place)
     first_pair, count = band(place)
 
-    def near_device(step):
-        other = lax.rem(near_me + step, near_count)
-        return (base + lax.div(other, 8), lax.rem(other, 8))
-
-    def far_device(step):
-        return (2 * lax.rem(chip_pair + step, far_count) + core, space)
-
     def member(kind, hop):
         where = lax.rem(row + hop + 4, 4)
         return kind * 4 + where, (base + kind, side * 4 + where)
@@ -199,12 +196,32 @@
     next_pair = lax.rem(seg + 2 * side - 2 * (1 - side) + nseg, nseg)
     across = (next_pair, space + 4 * (1 - side) - 4 * side)
 
+    def ring_device(step):
+        other = lax.rem(place + step, 8)
+        return (base + lax.div(other, 4), side * 4 + lax.rem(other, 4))
+
+    def side_device(step):
+        other = lax.rem(side_me + step, side_count)
+        pair = high * low_count + lax.rem(other, low_count)
+        return (2 * pair + core, lax.div(other, low_count) * 4 + row)
+
+    def far_device(step):
+        return (2 * (lax.rem(high + step, far_count) * low_count + low) + core, space)
+
+    rounds = [(8, ring_device), (side_count, side_device), (far_count, far_device)]
     barrier = pltpu.get_barrier_semaphore()
-    for step in range(1, near_count):
-        pl.semaphore_signal(barrier, inc=1, device_id=near_device(step), device_id_type=MESH)
-    pl.semaphore_signal(barrier, inc=1, device_id=across, device_id_type=MESH)
-    for step in range(1, far_count):
-        pl.semaphore_signal(barrier, inc=1, device_id=far_device(step), device_id_type=MESH)
+
+    def greet(device):
+        pl.semaphore_signal(barrier, inc=1, device_id=device, device_id_type=MESH)
+
+    @pl.when(traded)
+    def _():
+        greet(trader)
+
+    for size, device in rounds:
+        for step in range(1, size):
+            greet(device(step))
+    greet(across)
 
     own = [states.at[0], panel.at[0, 0], panel.at[0, 1]]
 
@@ -226,7 +243,7 @@
         pltpu.make_async_copy(src, dst, in_sem.at[index])
         for index, (src, dst) in enumerate(loads)
     ]
-    begins = [(own[group], fields.at[group_rows(group)]) for group in range(3)] + [(wall, wall_v)]
+    begins = [(wall, wall_v)] + [(own[group], fields.at[group_rows(group)]) for group in range(3)]
 
     @pl.when(jnp.logical_not(traded))
     def _():
@@ -235,7 +252,16 @@
 
     for load in loads:
         load.start()
-    pl.semaphore_wait(barrier, near_count + far_count - 1)
+    greetings = sum(size - 1 for size, _ in rounds) + 1
+
+    @pl.when(traded)
+    def _():
+        pl.semaphore_wait(barrier, greetings + 1)
+
+    @pl.when(jnp.logical_not(traded))
+    def _():
+        pl.semaphore_wait(barrier, greetings)
+
 
     def send(src, dst, send_sem, recv_sem, device):
         pltpu.make_async_remote_copy(
@@ -248,11 +274,13 @@
         ).start()
 
     def send_tiles(src, dst, three, send_sem, recv_sem, device):
-        send(src(0, 2), dst(0, 2), send_sem, recv_sem, device)
-
         @pl.when(three)
         def _():
-            send(src(2, 1), dst(2, 1), send_sem, recv_sem, device)
+            send(src(3), dst(3), send_sem, recv_sem, device)
+
+        @pl.when(jnp.logical_not(three))
+        def _():
+            send(src(2), dst(2), send_sem, recv_sem, device)
 
     @pl.when(traded)
     def _():
@@ -260,103 +288,93 @@
             send(src, dst, trade_send.at[index], trade_recv.at[index], trader)
 
     def slot(ref, *index):
-        return lambda start, tiles: ref.at[(*index, pl.ds(start * TILE, tiles * TILE))]
+        return lambda tiles: ref.at[(*index, pl.ds(0, tiles * TILE))]
 
     def band_of(ref, first, *index):
-        return lambda start, tiles: ref.at[(*index, tile_at(first + start, tiles))]
+        return lambda tiles: ref.at[(*index, tile_at(first, tiles))]
 
     everything = slice(None)
     direct = [(1 - core, 0), (0, 1), (1, 1), (0, 3), (1, 3)]
     opposite = [(0, 1), (1, 3)]
 
-    def send_heights(unit, group, source):
-        sems = out_send.at[unit, group]
+    def send_heights(group):
+        source = (pack, everything, group_rows(group), everything)
         for way, (kind, hop) in enumerate(opposite):
             other, _ = member(kind, 2)
             _, relay = member(core, hop)
             other_first, other_count = band(other)
             send_tiles(
-                band_of(source, other_first, everything, everything),
-                slot(passing, unit, group, way, everything, everything),
+                band_of(source[0], other_first, *source[1:]),
+                slot(passing, group, way, everything, everything, everything),
                 other_count == 3,
-                sems,
-                pass_recv.at[unit, group, way],
+                out_send.at[group],
+                pass_recv.at[group, way],
                 relay,
             )
         for kind, hop in direct:
             other, device = member(kind, hop)
             other_first, other_count = band(other)
             send_tiles(
-                band_of(source, other_first, everything, everything),
-                slot(got, unit, group, everything, place, everything),
+                band_of(source[0], other_first, *source[1:]),
+                slot(got, group, everything, everything, place, everything),
                 other_count == 3,
-                sems,
-                out_recv.at[unit, group],
+                out_send.at[group],
+                out_recv.at[group],
                 device,
             )
 
     def drain_tiles(ref, three, sem):
         @pl.when(three)
         def _():
-            drain(ref(0, 3), sem)
+            drain(ref(3), sem)
 
         @pl.when(jnp.logical_not(three))
         def _():
-            drain(ref(0, 2), sem)
-
-    def pass_heights(unit, group):
+            drain(ref(2), sem)
+
+    def pass_heights(group):
         for way, (kind, hop) in enumerate(opposite):
             origin, _ = member(core, hop + 2)
             other, device = member(kind, hop)
             _, other_count = band(other)
-            held = slot(passing, unit, group, way, everything, everything)
-            drain_tiles(held, other_count == 3, pass_recv.at[unit, group, way])
+            held = slot(passing, group, way, everything, everything, everything)
+            drain_tiles(held, other_count == 3, pass_recv.at[group, way])
             send_tiles(
                 held,
-                slot(got, unit, group, everything, origin, everything),
+                slot(got, group, everything, everything, origin, everything),
                 other_count == 3,
-                pass_send.at[unit, group, way],
-                out_recv.at[unit, group],
+                pass_send.at[group, way],
+                out_recv.at[group],
                 device,
             )
 
-    def keep_heights(unit, group, source):
-        got[unit, group, :, place, :, pl.ds(0, 2 * TILE)] = source[
-            group_rows(group), :, tile_at(first_pair, 2)
-        ]
-
-        @pl.when(count == 3)
-        def _():
-            got[unit, group, :, place, :, pl.ds(2 * TILE, TILE)] = source[
-                group_rows(group), :, tile_at(first_pair + 2)
+    def keep_heights(group):
+        for unit in range(2):
+            got[group, unit, :, place, :, pl.ds(0, 2 * TILE)] = pack[
+                unit, group_rows(group), :, tile_at(first_pair, 2)
             ]
+
+            @pl.when(count == 3)
+            def _():
+                got[group, unit, :, place, :, pl.ds(2 * TILE, TILE)] = pack[
+                    unit, group_rows(group), :, tile_at(first_pair + 2)
+                ]
 
     def drain(ref, sem):
         pltpu.make_async_copy(ref, ref, sem).wait()
 
-    def wait_heights(unit, group):
+    def wait_heights(group):
+        arrived = slot(got, group, everything, everything, pl.ds(0, 7), everything)
+        drain_tiles(arrived, count == 3, out_recv.at[group])
+
+    def wait_pairs(ref, sem):
         @pl.when(count == 3)
         def _():
-            drain(
-                got.at[unit, group, :, pl.ds(0, 7), :, pl.ds(0, 3 * TILE)],
-                out_recv.at[unit, group],
-            )
+            drain(ref.at[..., pl.ds(0, (PAIRS - 3) * TILE)], sem)
 
         @pl.when(count == 2)
         def _():
-            drain(
-                got.at[unit, group, :, pl.ds(0, 7), :, pl.ds(0, 2 * TILE)],
-                out_recv.at[unit, group],
-            )
-
-    def wait_pairs(sem):
-        @pl.when(count == 3)
-        def _():
-            drain(returned.at[0, :, :, pl.ds(0, (PAIRS - 3) * TILE)], sem)
-
-        @pl.when(count == 2)
-        def _():
-            drain(returned.at[0, :, :, pl.ds(0, (PAIRS - 2) * TILE)], sem)
+            drain(ref.at[..., pl.ds(0, (PAIRS - 2) * TILE)], sem)
 
     def across_heights(group, source, other, coefficient, target):
         rows = pl.ds(3 * group, 3)
@@ -382,11 +400,7 @@
             target[rows, :, lanes] = pltpu.roll(source[rows, :, lanes], NZ, 2)
 
     def begin(group):
-        drain(fields.at[group_rows(group)], trade_recv.at[group])
-        send_heights(0, group, fields.at[group_rows(group)])
-        keep_heights(0, group, fields)
-
-    def differentiate(group):
+        drain(fields.at[group_rows(group)], trade_recv.at[1 + group])
         turn(group, fields, swapped)
         across_heights(
             group,
@@ -395,31 +409,17 @@
             lambda pair, row: derivative[pair, pl.ds(row, 1), :],
             slopes,
         )
-
-    def send_slopes(group):
-        send_heights(1, group, slopes.at[group_rows(group)])
-        keep_heights(1, group, slopes)
-
-    def send_start(sources, device):
-        for group in range(3):
-            send(
-                sources[group],
-                later.at[group_rows(group)],
-                later_send.at[group],
-                later_recv.at[group],
-                device,
-            )
+        send_heights(group)
+        keep_heights(group)
 
     def shift():
-        mine = [fields.at[group_rows(group)] for group in range(3)]
-
         @pl.when(side == 0)
         def _():
-            send_start(mine, across)
+            send(fields, later, later_send, later_recv, across)
 
         @pl.when(core * side == 1)
         def _():
-            send_start(mine, (seg, space - 4))
+            send(fields, later, later_send, later_recv, (seg, space - 4))
 
         @pl.when(core * (1 - side) == 1)
         def _():
@@ -428,7 +428,7 @@
                     own[group],
                     later.at[group_rows(group)],
                     home_send.at[3 + group],
-                    later_recv.at[group],
+                    later_recv,
                     (seg - 1, space),
                 )
 
@@ -456,11 +456,10 @@
         return jnp.concatenate([rows, rows], axis=1) * damping[...]
 
     def transform(group):
-        wait_heights(0, group)
-        wait_heights(1, group)
+        wait_heights(group)
 
         def modes(unit):
-            value = got[unit, group].reshape(3, NX, 3 * TILE)
+            value = got[group, unit].reshape(3, NX, 3 * TILE)
             return stacked(jnp.concatenate([value[0], value[1], value[2]], axis=1), 0)
 
         def by_rows(value):
@@ -563,7 +562,7 @@
             )
 
     def finish(group, keep):
-        wait_pairs(back_recv.at[group])
+        wait_pairs(returned.at[0], back_recv.at[group])
         rows = group_rows(group)
         for pair in range(PAIRS):
             lanes = pl.ds(pair * TILE, TILE)
@@ -573,7 +572,8 @@
         across_heights(
             group, forced, turned, lambda pair, row: solve[pair, row], ends
         )
-        drain(later.at[rows], later_recv.at[group])
+        if group == 0:
+            drain(later, later_recv)
         gap = ends[rows] - later[rows]
         gaps[rows] = gap
 
@@ -591,29 +591,20 @@
         def _():
             gaps_home[rows] = gap
 
+    drain(wall_v, trade_recv.at[0])
+    lax.fori_loop(0, PAIRS, solve_rows, 0)
+    loads[0].wait()
     begin(0)
-    loads[0].wait()
-    differentiate(0)
-    send_slopes(0)
-    pass_heights(0, 0)
     begin(1)
-    differentiate(1)
-    pass_heights(1, 0)
-    send_slopes(1)
-    drain(wall_v, trade_recv.at[3])
-    lax.fori_loop(0, PAIRS, solve_rows, 0)
-    pass_heights(0, 1)
+    pass_heights(0)
     begin(2)
-    differentiate(2)
-    pass_heights(1, 1)
-    send_slopes(2)
     shift()
+    pass_heights(1)
     for load in loads[1:]:
         load.wait()
     keep = kept()
-    pass_heights(0, 2)
     transform(0)
-    pass_heights(1, 2)
+    pass_heights(2)
     transform(1)
     pass_back(0)
     transform(2)
@@ -663,8 +654,9 @@
             drain(slots.at[pl.ds(0, size - 1)], sum_recv.at[which])
         return jnp.sum(slots[...], axis=0)
 
-    message = exchange(0, near, near_me, near_count, near_device, message)
-    message = exchange(1, far, chip_pair, far_count, far_device, message)
+    slots = [ring_sums, side_sums, far_sums]
+    for which, me in enumerate([place, side_me, high]):
+        message = exchange(which, slots[which], me, *rounds[which], message)
 
     def number(index):
         return message[:, index : index + 1]
@@ -697,9 +689,8 @@
 
     lax.fori_loop(0, PAIRS, write, 0)
 
-    for unit in range(2):
-        for group in range(3):
-            wait_pairs(out_send.at[unit, group])
+    for group in range(3):
+        wait_pairs(pack.at[:, pl.ds(0, 3)], out_send.at[group])
     for group in range(3):
         @pl.when(count == 3)
         def _():
@@ -715,12 +706,11 @@
             _, other_count = band(other)
             origin, _ = member(core, hop + 2)
             _, origin_count = band(origin)
-            for unit in range(2):
-                drain_tiles(
-                    slot(passing, unit, group, way, everything, everything),
-                    other_count == 3,
-                    pass_send.at[unit, group, way],
-                )
+            drain_tiles(
+                slot(passing, group, way, everything, everything, everything),
+                other_count == 3,
+                pass_send.at[group, way],
+            )
             drain_tiles(
                 slot(passing_back, group, way, everything, everything),
                 origin_count == 3,
@@ -730,23 +720,22 @@
     @pl.when(traded)
     def _():
         for group in range(3):
-            drain(fields.at[group_rows(group)], trade_send.at[group])
+            drain(fields.at[group_rows(group)], trade_send.at[1 + group])
             drain(gaps.at[group_rows(group)], home_send.at[group])
-        drain(wall_v, trade_send.at[3])
+        drain(wall_v, trade_send.at[0])
 
     @pl.when(jnp.logical_or(side == 0, core * side == 1))
     def _():
-        for group in range(3):
-            drain(fields.at[group_rows(group)], later_send.at[group])
+        drain(later, later_send)
 
     @pl.when(core * (1 - side) == 1)
     def _():
         for group in range(3):
             drain(home.at[group_rows(group)], home_send.at[3 + group])
 
-    drain(near.at[pl.ds(0, near_count - 1)], sum_send.at[0])
-    if far_count > 1:
-        drain(far.at[pl.ds(0, far_count - 1)], sum_send.at[1])
+    for which, (size, _) in enumerate(rounds):
+        if size > 1:
+            drain(slots[which].at[pl.ds(0, size - 1)], sum_send.at[which])
 
 
 def local(nseg, constants, states, tangent_panel, wall_inverse, keep_mask):
@@ -764,34 +753,37 @@
         *[pltpu.VMEM(value.shape, value.dtype) for value in constants],
         pltpu.VMEM((8 * NY, NY), f32),
         pltpu.VMEM((NX, NZ), jnp.int32),
-        *[pltpu.VMEM(whole, f32)] * 4,
-        pltpu.VMEM((2, 3, 3, 8, 8, 3 * TILE), f32),
-        pltpu.VMEM((2, 3, 2, 3, 8, 3 * TILE), f32),
+        pltpu.VMEM(whole, f32),
+        pltpu.VMEM((2, *whole), f32),
+        pltpu.VMEM(whole, f32),
+        pltpu.VMEM((3, 2, 3, 8, 8, 3 * TILE), f32),
+        pltpu.VMEM((3, 2, 2, 3, 8, 3 * TILE), f32),
         pltpu.VMEM((3, 12, NX, TILE), f32),
         pltpu.VMEM((3, 3, NX, 3 * TILE), f32),
         pltpu.VMEM((3, 2, 3, 8, 3 * TILE), f32),
         pltpu.VMEM((3, 3, 8, LANES), f32),
         pltpu.VMEM((PAIRS, 2 * PAIRS, 8, TILE), f32),
         *[pltpu.VMEM(whole, f32)] * 6,
-        pltpu.VMEM((16, 1, TILE), f32),
-        pltpu.VMEM((nseg // 2, 1, TILE), f32),
+        pltpu.VMEM((8, 1, TILE), f32),
+        pltpu.VMEM((2 * min(4, nseg // 2), 1, TILE), f32),
+        pltpu.VMEM((nseg // 2 // min(4, nseg // 2), 1, TILE), f32),
         sem((11,)),
         sem((4,)),
         sem((4,)),
-        sem((2, 3)),
-        sem((2, 3)),
-        sem((2, 3, 2)),
-        sem((2, 3, 2)),
         sem((3,)),
         sem((3,)),
         sem((3, 2)),
         sem((3, 2)),
         sem((3,)),
         sem((3,)),
+        sem((3, 2)),
+        sem((3, 2)),
+        sem,
+        sem,
         sem((6,)),
         sem((3,)),
-        sem((2,)),
-        sem((2,)),
+        sem((3,)),
+        sem((3,)),
     ]
     return pl.pallas_call(
         functools.partial(kernel, nseg),

time: 73.5 us -> 71.2 us (0.969)
  Pallas kernels: 70.1 us -> 68 us
    pallas_call x1, Pallas kernels: 70.1 us -> 68 us  [local(): pl.pallas_call(functools.partial(kernel, nseg), out_shape=[jax.ShapeDtype...]
where the time goes in v5:
time: 71.2 us; the launch traced here: 71 us
  Pallas kernels  68 us (96%)
  local copies, waits for them, and re-layouts  2.39 us (3%)
    pallas_call x1, Pallas kernels, local(): pl.pallas_call(functools.partial(kernel, nseg), out_shape=[jax.ShapeDtype...  68 us
    unnamed x4, local copies, waits for them, and re-layouts  2.39 us

profile of v5, /device:TPU:1, one launch (start us, length us, event | category | flops | bytes accessed | tf_op | source)
XLA Modules:
  0.0 71.0 jit_solution(15767755214606040994)
XLA Ops:
  0.6 68.0 %newton_step.1 = (f32[1,3,8,2560]{3,2,1,0:T(8,128)}, f32[1,3,8,2560]{3,2,1,0:T(8,128)}) custom-call(f32[1,3,8,2560]{3,2,1,0:T(8,128)} %states.1, f32[1,2,3,8,2560]{4,3,2,1,0:T(8,128)} %panel.1, f32[320,40]{1,0:T(8,128)} %bitcast.1, s32[64,64]{1,0:T(8,128)} %mask.1, bf16[128,192]{1,0:T(8,128)(2,1)} %constant.14.clone.x_forward_in, ...), custom_call_target="tpu_custom_call" | custom-call | tf_op jit(solution)/shard_map/newton_step/pallas_call | solution.py:788
  68.6 0.0 copy-start
  68.6 1.7 %copy.15 = f32[1,3,8,2560]{3,2,1,0:T(8,128)} copy(f32[1,3,8,2560]{3,2,1,0:T(8,128)} %get-tuple-element.4) | data formatting | bytes 491520
  70.3 0.0 copy-done
  70.3 0.7 copy.16
Async XLA Ops:
  68.6 1.7 %copy-start = (f32[1,3,8,2560]{3,2,1,0:T(8,128)S(1)}, f32[1,3,8,2560]{3,2,1,0:T(8,128)}, u32[]{:S(2)}) copy-start(f32[1,3,8,2560]{3,2,1,0:T(8,128)} %get-tuple-element.5) | copy-start | bytes 737284

commit v6 on v5

--- a/solution.py
+++ b/solution.py
@@ -123,8 +123,8 @@
     derivative_in,
     heights_in,
     damping_in,
-    corrected,
-    new_residual,
+    gaps_home,
+    weights,
     x_forward,
     x_back,
     z_forward,
@@ -134,7 +134,6 @@
     damping,
     wall_v,
     mask_v,
-    home,
     pack,
     swapped,
     got,
@@ -149,7 +148,6 @@
     ends,
     later,
     gaps,
-    gaps_home,
     ring_sums,
     side_sums,
     far_sums,
@@ -218,7 +216,7 @@
     def _():
         greet(trader)
 
-    for size, device in rounds:
+    for size, device in reversed(rounds):
         for step in range(1, size):
             greet(device(step))
     greet(across)
@@ -237,13 +235,12 @@
         (z_back_in, z_back),
         (heights_in, heights),
         (damping_in, damping),
-        *[(own[group], home.at[group_rows(group)]) for group in range(3)],
     ]
     loads = [
         pltpu.make_async_copy(src, dst, in_sem.at[index])
         for index, (src, dst) in enumerate(loads)
     ]
-    begins = [(wall, wall_v)] + [(own[group], fields.at[group_rows(group)]) for group in range(3)]
+    begins = [(own[group], fields.at[group_rows(group)]) for group in range(3)] + [(wall, wall_v)]
 
     @pl.when(jnp.logical_not(traded))
     def _():
@@ -400,7 +397,7 @@
             target[rows, :, lanes] = pltpu.roll(source[rows, :, lanes], NZ, 2)
 
     def begin(group):
-        drain(fields.at[group_rows(group)], trade_recv.at[1 + group])
+        drain(fields.at[group_rows(group)], trade_recv.at[group])
         turn(group, fields, swapped)
         across_heights(
             group,
@@ -589,16 +586,18 @@
 
         @pl.when(jnp.logical_not(traded))
         def _():
-            gaps_home[rows] = gap
-
-    drain(wall_v, trade_recv.at[0])
-    lax.fori_loop(0, PAIRS, solve_rows, 0)
+            pltpu.make_async_copy(
+                gaps.at[rows], gaps_home.at[rows], home_recv.at[group]
+            ).start()
+
     loads[0].wait()
     begin(0)
     begin(1)
     pass_heights(0)
     begin(2)
     shift()
+    drain(wall_v, trade_recv.at[3])
+    lax.fori_loop(0, PAIRS, solve_rows, 0)
     pass_heights(1)
     for load in loads[1:]:
         load.wait()
@@ -666,29 +665,11 @@
     diag = [number(2) + border[0] * border[0], number(3) + border[1] * border[1]]
     first = [-number(4) / diag[0], -number(5) / diag[1]]
     cross = number(6) + border[0] * border[1]
-    weight = [
-        first[0] - first[1] * cross / diag[0],
-        first[1] - first[0] * cross / diag[1],
-    ]
-    weight = [jnp.broadcast_to(value, (8, TILE)) for value in weight]
-
-    @pl.when(traded)
-    def _():
-        for group in range(3):
-            drain(gaps_home.at[group_rows(group)], home_recv.at[group])
-
-    def write(index, carry):
-        lanes = tile_at(index)
-        for source, target in ((home, corrected), (gaps_home, new_residual)):
-            target[0, :, :, lanes] = (
-                source[pl.ds(0, 3), :, lanes]
-                + weight[0] * source[pl.ds(3, 3), :, lanes]
-                + weight[1] * source[pl.ds(6, 3), :, lanes]
-            )
-        return carry
-
-    lax.fori_loop(0, PAIRS, write, 0)
-
+    weights[pl.ds(0, 1), :] = jnp.broadcast_to(first[0] - first[1] * cross / diag[0], (1, TILE))
+    weights[pl.ds(1, 1), :] = jnp.broadcast_to(first[1] - first[0] * cross / diag[1], (1, TILE))
+
+    for group in range(3):
+        drain(gaps_home.at[group_rows(group)], home_recv.at[group])
     for group in range(3):
         wait_pairs(pack.at[:, pl.ds(0, 3)], out_send.at[group])
     for group in range(3):
@@ -720,9 +701,9 @@
     @pl.when(traded)
     def _():
         for group in range(3):
-            drain(fields.at[group_rows(group)], trade_send.at[1 + group])
+            drain(fields.at[group_rows(group)], trade_send.at[group])
             drain(gaps.at[group_rows(group)], home_send.at[group])
-        drain(wall_v, trade_send.at[0])
+        drain(wall_v, trade_send.at[3])
 
     @pl.when(jnp.logical_or(side == 0, core * side == 1))
     def _():
@@ -731,11 +712,26 @@
     @pl.when(core * (1 - side) == 1)
     def _():
         for group in range(3):
-            drain(home.at[group_rows(group)], home_send.at[3 + group])
+            drain(fields.at[group_rows(group)], home_send.at[3 + group])
 
     for which, (size, _) in enumerate(rounds):
         if size > 1:
             drain(slots[which].at[pl.ds(0, size - 1)], sum_send.at[which])
+
+
+def final_kernel(states, panel, gaps, weights, corrected, new_residual):
+    a = jnp.broadcast_to(weights[pl.ds(0, 1), :], (8, TILE))
+    b = jnp.broadcast_to(weights[pl.ds(1, 1), :], (8, TILE))
+    for pair in range(PAIRS):
+        lanes = pl.ds(pair * TILE, TILE)
+        corrected[0, :, :, lanes] = (
+            states[0, :, :, lanes] + a * panel[0, 0, :, :, lanes] + b * panel[0, 1, :, :, lanes]
+        )
+        new_residual[0, :, :, lanes] = (
+            gaps[pl.ds(0, 3), :, lanes]
+            + a * gaps[pl.ds(3, 3), :, lanes]
+            + b * gaps[pl.ds(6, 3), :, lanes]
+        )
 
 
 def local(nseg, constants, states, tangent_panel, wall_inverse, keep_mask):
@@ -753,7 +749,6 @@
         *[pltpu.VMEM(value.shape, value.dtype) for value in constants],
         pltpu.VMEM((8 * NY, NY), f32),
         pltpu.VMEM((NX, NZ), jnp.int32),
-        pltpu.VMEM(whole, f32),
         pltpu.VMEM((2, *whole), f32),
         pltpu.VMEM(whole, f32),
         pltpu.VMEM((3, 2, 3, 8, 8, 3 * TILE), f32),
@@ -763,11 +758,11 @@
         pltpu.VMEM((3, 2, 3, 8, 3 * TILE), f32),
         pltpu.VMEM((3, 3, 8, LANES), f32),
         pltpu.VMEM((PAIRS, 2 * PAIRS, 8, TILE), f32),
-        *[pltpu.VMEM(whole, f32)] * 6,
+        *[pltpu.VMEM(whole, f32)] * 5,
         pltpu.VMEM((8, 1, TILE), f32),
         pltpu.VMEM((2 * min(4, nseg // 2), 1, TILE), f32),
         pltpu.VMEM((nseg // 2 // min(4, nseg // 2), 1, TILE), f32),
-        sem((11,)),
+        sem((8,)),
         sem((4,)),
         sem((4,)),
         sem((3,)),
@@ -785,17 +780,31 @@
         sem((3,)),
         sem((3,)),
     ]
-    return pl.pallas_call(
+    vmem, hbm = pl.BlockSpec(memory_space=pltpu.VMEM), pl.BlockSpec(memory_space=pl.ANY)
+    grant = 64 * 1024 * 1024
+    gaps, weights = pl.pallas_call(
         functools.partial(kernel, nseg),
-        out_shape=[jax.ShapeDtypeStruct((1, 3, 8, LANES), f32)] * 2,
-        in_specs=[pl.BlockSpec(memory_space=pl.ANY)] * len(operands),
-        out_specs=[pl.BlockSpec(memory_space=pltpu.VMEM)] * 2,
+        out_shape=[
+            jax.ShapeDtypeStruct(whole, f32),
+            jax.ShapeDtypeStruct((2, TILE), f32),
+        ],
+        in_specs=[hbm] * len(operands),
+        out_specs=[hbm, vmem],
         scratch_shapes=scratch,
         compiler_params=pltpu.CompilerParams(
-            collective_id=0, has_side_effects=True, vmem_limit_bytes=64 * 1024 * 1024
+            collective_id=0, has_side_effects=True, vmem_limit_bytes=grant
         ),
         name="newton_step",
     )(*operands)
+    result = jax.ShapeDtypeStruct((1, 3, 8, LANES), f32)
+    return pl.pallas_call(
+        final_kernel,
+        out_shape=[result, result],
+        in_specs=[vmem] * 4,
+        out_specs=[vmem, vmem],
+        compiler_params=pltpu.CompilerParams(vmem_limit_bytes=grant),
+        name="newton_final",
+    )(states, tangent_panel, gaps, weights)
 
 
 def solution(mesh):

time: 71.2 us -> 71.5 us (level)
  Pallas kernels: 68 us -> 70.7 us
  local copies, waits for them, and re-layouts: 2.39 us -> 0 us
    unnamed x4 -> x0, local copies, waits for them, and re-layouts: 2.39 us -> none
    pallas_call x0 -> x1, Pallas kernels: none -> 2.23 us  [local(): pl.pallas_call(final_kernel, out_shape=[result, result], in_specs=[vmem]...]
where the time goes in v6:
time: 71.5 us; the launch traced here: 71.3 us
  Pallas kernels  70.7 us (99%)
    pallas_call x1, Pallas kernels, local(): pl.pallas_call(functools.partial(kernel, nseg), out_shape=[jax.ShapeDtype...  68.5 us
    pallas_call x1, Pallas kernels, local(): pl.pallas_call(final_kernel, out_shape=[result, result], in_specs=[vmem]...  2.23 us

profile of v6, /device:TPU:1, one launch (start us, length us, event | category | flops | bytes accessed | tf_op | source)
XLA Modules:
  0.0 71.3 jit_solution(9559436797596160213)
XLA Ops:
  0.6 68.5 %newton_step.1 = (f32[9,8,2560]{2,1,0:T(8,128)}, f32[2,128]{1,0:T(2,128)}) custom-call(f32[1,3,8,2560]{3,2,1,0:T(8,128)} %states.3, f32[1,2,3,8,2560]{4,3,2,1,0:T(8,128)} %panel.3, f32[320,40]{1,0:T(8,128)} %bitcast.1, s32[64,64]{1,0:T(8,128)} %mask.1, bf16[128,192]{1,0:T(8,128)(2,1)} %constant.14.clone.x_forward_in, ...), custom_call_target="tpu_custom_call" | custom-call | tf_op jit(solution)/shard_map/newton_step/pallas_call | solution.py:785
  69.1 2.2 %newton_final.1 = (f32[1,3,8,2560]{3,2,1,0:T(8,128)}, f32[1,3,8,2560]{3,2,1,0:T(8,128)}) custom-call(f32[1,3,8,2560]{3,2,1,0:T(8,128)} %states.3, f32[1,2,3,8,2560]{4,3,2,1,0:T(8,128)} %panel.3, f32[9,8,2560]{2,1,0:T(8,128)} %get-tuple-element.4.gaps, f32[2,128]{1,0:T(2,128)} %get-tuple-element.5.weights), custom_call_target="tpu_custom_call" | custom-call | tf_op jit(solution)/shard_map/newton_final/pallas_call | solution.py:800

commit v7 on v5

--- a/solution.py
+++ b/solution.py
@@ -138,10 +138,8 @@
     pack,
     swapped,
     got,
-    passing,
     flow,
     outgoing,
-    passing_back,
     returned,
     solve,
     forced,
@@ -158,12 +156,8 @@
     trade_recv,
     out_send,
     out_recv,
-    pass_send,
-    pass_recv,
     back_send,
     back_recv,
-    pass_back_send,
-    pass_back_recv,
     later_send,
     later_recv,
     home_send,
@@ -294,23 +288,10 @@
         return lambda tiles: ref.at[(*index, tile_at(first, tiles))]
 
     everything = slice(None)
-    direct = [(1 - core, 0), (0, 1), (1, 1), (0, 3), (1, 3)]
-    opposite = [(0, 1), (1, 3)]
+    direct = [(0, 2), (1, 2), (0, 1), (1, 1), (0, 3), (1, 3), (1 - core, 0)]
 
     def send_heights(group):
         source = (pack, everything, group_rows(group), everything)
-        for way, (kind, hop) in enumerate(opposite):
-            other, _ = member(kind, 2)
-            _, relay = member(core, hop)
-            other_first, other_count = band(other)
-            send_tiles(
-                band_of(source[0], other_first, *source[1:]),
-                slot(passing, group, way, everything, everything, everything),
-                other_count == 3,
-                out_send.at[group],
-                pass_recv.at[group, way],
-                relay,
-            )
         for kind, hop in direct:
             other, device = member(kind, hop)
             other_first, other_count = band(other)
@@ -331,22 +312,6 @@
         @pl.when(jnp.logical_not(three))
         def _():
             drain(ref(2), sem)
-
-    def pass_heights(group):
-        for way, (kind, hop) in enumerate(opposite):
-            origin, _ = member(core, hop + 2)
-            other, device = member(kind, hop)
-            _, other_count = band(other)
-            held = slot(passing, group, way, everything, everything, everything)
-            drain_tiles(held, other_count == 3, pass_recv.at[group, way])
-            send_tiles(
-                held,
-                slot(got, group, everything, everything, origin, everything),
-                other_count == 3,
-                pass_send.at[group, way],
-                out_recv.at[group],
-                device,
-            )
 
     def keep_heights(group):
         for unit in range(2):
@@ -512,17 +477,6 @@
         def rows_of(other):
             return pl.ds(pl.multiple_of(other * 8, 8), 8)
 
-        for way, (kind, hop) in enumerate(opposite):
-            other, _ = member(kind, 2)
-            _, relay = member(core, hop)
-            send_tiles(
-                slot(outgoing, group, everything, rows_of(other)),
-                slot(passing_back, group, way, everything, everything),
-                count == 3,
-                back_send.at[group],
-                pass_back_recv.at[group, way],
-                relay,
-            )
         for kind, hop in direct:
             other, device = member(kind, hop)
             send_tiles(
@@ -544,22 +498,6 @@
             returned[group, :, :, tile_at(first_pair + 2)] = outgoing[
                 group, :, mine, pl.ds(2 * TILE, TILE)
             ]
-
-    def pass_back(group):
-        for way, (kind, hop) in enumerate(opposite):
-            origin, _ = member(core, hop + 2)
-            _, device = member(kind, hop)
-            origin_first, origin_count = band(origin)
-            held = slot(passing_back, group, way, everything, everything)
-            drain_tiles(held, origin_count == 3, pass_back_recv.at[group, way])
-            send_tiles(
-                held,
-                band_of(returned, origin_first, group, everything, everything),
-                origin_count == 3,
-                pass_back_send.at[group, way],
-                back_recv.at[group],
-                device,
-            )
 
     def finish(group, keep):
         wait_pairs(returned.at[0], back_recv.at[group])
@@ -596,21 +534,15 @@
     loads[0].wait()
     begin(0)
     begin(1)
-    pass_heights(0)
     begin(2)
     shift()
-    pass_heights(1)
     for load in loads[1:]:
         load.wait()
     keep = kept()
     transform(0)
-    pass_heights(2)
     transform(1)
-    pass_back(0)
     transform(2)
-    pass_back(1)
     finish(0, keep)
-    pass_back(2)
     finish(1, keep)
     finish(2, keep)
 
@@ -699,23 +631,6 @@
         @pl.when(count == 2)
         def _():
             drain(outgoing.at[group, :, pl.ds(0, 56), pl.ds(0, 2 * TILE)], back_send.at[group])
-
-    for group in range(3):
-        for way, (kind, hop) in enumerate(opposite):
-            other, _ = member(kind, hop)
-            _, other_count = band(other)
-            origin, _ = member(core, hop + 2)
-            _, origin_count = band(origin)
-            drain_tiles(
-                slot(passing, group, way, everything, everything, everything),
-                other_count == 3,
-                pass_send.at[group, way],
-            )
-            drain_tiles(
-                slot(passing_back, group, way, everything, everything),
-                origin_count == 3,
-                pass_back_send.at[group, way],
-            )
 
     @pl.when(traded)
     def _():
@@ -757,10 +672,8 @@
         pltpu.VMEM((2, *whole), f32),
         pltpu.VMEM(whole, f32),
         pltpu.VMEM((3, 2, 3, 8, 8, 3 * TILE), f32),
-        pltpu.VMEM((3, 2, 2, 3, 8, 3 * TILE), f32),
         pltpu.VMEM((3, 12, NX, TILE), f32),
         pltpu.VMEM((3, 3, NX, 3 * TILE), f32),
-        pltpu.VMEM((3, 2, 3, 8, 3 * TILE), f32),
         pltpu.VMEM((3, 3, 8, LANES), f32),
         pltpu.VMEM((PAIRS, 2 * PAIRS, 8, TILE), f32),
         *[pltpu.VMEM(whole, f32)] * 6,
@@ -772,12 +685,8 @@
         sem((4,)),
         sem((3,)),
         sem((3,)),
-        sem((3, 2)),
-        sem((3, 2)),
         sem((3,)),
         sem((3,)),
-        sem((3, 2)),
-        sem((3, 2)),
         sem,
         sem,
         sem((6,)),

time: 71.2 us -> 68.9 us (0.968)
  Pallas kernels: 68 us -> 65.7 us
    pallas_call x1, Pallas kernels: 68 us -> 65.7 us  [local(): pl.pallas_call(functools.partial(kernel, nseg), out_shape=[jax.ShapeDtype...]
where the time goes in v7:
time: 68.9 us; the launch traced here: 68.7 us
  Pallas kernels  65.7 us (95%)
  local copies, waits for them, and re-layouts  2.39 us (3%)
    pallas_call x1, Pallas kernels, local(): pl.pallas_call(functools.partial(kernel, nseg), out_shape=[jax.ShapeDtype...  65.7 us
    unnamed x4, local copies, waits for them, and re-layouts  2.39 us

profile of v7, /device:TPU:1, one launch (start us, length us, event | category | flops | bytes accessed | tf_op | source)
XLA Modules:
  0.0 68.7 jit_solution(6728204763593915460)
XLA Ops:
  0.6 65.7 %newton_step.1 = (f32[1,3,8,2560]{3,2,1,0:T(8,128)}, f32[1,3,8,2560]{3,2,1,0:T(8,128)}) custom-call(f32[1,3,8,2560]{3,2,1,0:T(8,128)} %states.1, f32[1,2,3,8,2560]{4,3,2,1,0:T(8,128)} %panel.1, f32[320,40]{1,0:T(8,128)} %bitcast.1, s32[64,64]{1,0:T(8,128)} %mask.1, bf16[128,192]{1,0:T(8,128)(2,1)} %constant.14.clone.x_forward_in, ...), custom_call_target="tpu_custom_call" | custom-call | tf_op jit(solution)/shard_map/newton_step/pallas_call | solution.py:697
  66.3 0.0 copy-start
  66.3 1.7 %copy.15 = f32[1,3,8,2560]{3,2,1,0:T(8,128)} copy(f32[1,3,8,2560]{3,2,1,0:T(8,128)} %get-tuple-element.4) | data formatting | bytes 491520
  68.0 0.0 copy-done
  68.0 0.7 %copy.16 = f32[1,3,8,2560]{3,2,1,0:T(8,128)} copy(f32[1,3,8,2560]{3,2,1,0:T(8,128)S(1)} %copy-done) | data formatting | bytes 491520
Async XLA Ops:
  66.3 1.7 %copy-start = (f32[1,3,8,2560]{3,2,1,0:T(8,128)S(1)}, f32[1,3,8,2560]{3,2,1,0:T(8,128)}, u32[]{:S(2)}) copy-start(f32[1,3,8,2560]{3,2,1,0:T(8,128)} %get-tuple-element.5) | copy-start | bytes 737284
